TPU v7x, 512 devices: a whole 4x8x8 slice. The times are simulated.
512 devices in a mesh: dom: 128 (over y, z, core), sub: 4 (over x).
Axes of the slice: x: 4, y: 8, z: 8, core: 2. Of those that a mesh axis runs over, the one named last changes fastest.
Arguments:
- fine_nodes: bfloat16 [524288, 512], P(('dom', 'sub')), may hold values from -6 to 6
- edge_tiles: bfloat16 [28672, 128, 128], P(('dom', 'sub')), may hold values from -0.375 to 0.375
- edge_target: int32 [28672], P(('dom', 'sub')), may hold values from 0 to 7
- edge_source: int32 [28672], P(('dom', 'sub')), may hold values from 0 to 11, as said below
- edge_count: int32 [512], P(('dom', 'sub')), may hold values from 14 to 56, as said below
- halo_blocks: int32 [2048], P(('dom', 'sub')), may hold values from 0 to 7
- pool_owner: int32 [4096], P(('dom', 'sub')), may hold values from 0 to 127, as said below
- coarse_tiles: bfloat16 [1024, 128, 128], P(('dom', 'sub')), may hold values from -0.375 to 0.375
- pooled_block_source_index: int32 [1024], P(('dom', 'sub')), may hold values from 1 to 3
- fine_first: bfloat16 [1024, 512], replicated, may hold values from -0.1875 to 0.1875
- fine_bias: float32 [512], replicated, may hold values from -4 to 4
- fine_second: bfloat16 [512, 512], replicated, may hold values from -0.25 to 0.25
- fine_gain: float32 [512], replicated, may hold values from 0.1 to 1.9
- coarse_first: bfloat16 [1024, 512], replicated, may hold values from -0.1875 to 0.1875
- coarse_bias: float32 [512], replicated, may hold values from -4 to 4
- coarse_second: bfloat16 [512, 512], replicated, may hold values from -0.25 to 0.25
- pooled_level_scale_factor: float32 [512], replicated, may hold values from 0.1 to 1.9
Outputs:
- fine_out: bfloat16 [524288, 512], P(('dom', 'sub'))
Inputs may be any that keep to these rules, and one draw needn't show every extreme that they name: `edge_source`: entry e of a device's list reads block 8 + e of the source table for e below 4. `edge_count`: some device has all 56 entries live. `pool_owner`: a block's owner lies in the same aligned group of 4 dom indices as the block's device; every device receives exactly one tile of each block index k; one device sends at most 2 blocks to one owner, and some device does so.
All inputs are finite; a program needn't handle non-finite values.
Results may differ from a plain program's by a relative error of at most 0.0051.
Values may be sent and summed in bfloat16 or wider, within the bound.
No kernel may reach another device: no remote copies, remote signals or barrier semaphores. Data moves between devices by JAX's collectives and lax.ppermute only.
A program may use at most 128 MiB of HBM per device.

v0:
```python
import jax
import jax.numpy as jnp
from jax import lax
from jax.sharding import PartitionSpec as P

POOL = 8
WIN = 4


def passed_along(block, axis, distance):
    devices = range(lax.axis_size(axis))
    route = [(i - distance, i) for i in devices if i - distance in devices]
    return lax.ppermute(block, axis, route)


def layer_norm(values, gain_vec):
    row_mean = jnp.mean(values, axis=-1, keepdims=True)
    centred = values - row_mean
    variance = jnp.mean(centred * centred, axis=-1, keepdims=True)
    return centred * lax.rsqrt(variance + 1e-05) * gain_vec


def node_update(node_rows, messages, weight_in, bias_in, weight_out, gain_vec):
    joined = jnp.concatenate([node_rows, messages], axis=-1)
    hidden_act = jnp.maximum(
        jnp.dot(joined, weight_in, preferred_element_type=jnp.float32) + bias_in, 0.0
    )
    hidden_act = hidden_act.astype(jnp.bfloat16)
    projected = jnp.dot(hidden_act, weight_out, preferred_element_type=jnp.float32)
    return layer_norm(projected, gain_vec)


def select_rows(selector, values):
    return jnp.dot(
        selector.astype(jnp.bfloat16), values, preferred_element_type=jnp.float32
    ).astype(jnp.bfloat16)


def per_device(
    fine_nodes,
    edge_tiles,
    edge_target,
    edge_source,
    edge_count,
    halo_blocks,
    pool_owner,
    coarse_tiles,
    pooled_block_source_index,
    fine_first,
    fine_bias,
    fine_second,
    fine_gain,
    coarse_first,
    coarse_bias,
    coarse_second,
    pooled_level_scale_factor,
):
    block_count = pool_owner.shape[0]
    block_rows = edge_tiles.shape[1]
    feature_width = fine_nodes.shape[1]
    tile_rows = block_rows // POOL
    blocks = fine_nodes.reshape(block_count, block_rows, feature_width)
    slot_index = jnp.arange(block_count, dtype=jnp.int32)
    pooled = jnp.mean(
        fine_nodes.astype(jnp.float32).reshape(block_count, tile_rows, POOL, feature_width), axis=2
    )
    pooled = pooled.astype(jnp.bfloat16)
    flat_pooled = pooled.reshape(block_count, -1)
    dom_index = lax.axis_index("dom")
    capacity = max(1, block_count // WIN)
    shared = pool_owner[:, None] == pool_owner[None, :]
    earlier = slot_index[None, :] < slot_index[:, None]
    slot_rank = jnp.sum(jnp.where(shared & earlier, 1, 0), axis=1).astype(jnp.int32)
    cap_index = jnp.arange(capacity, dtype=jnp.int32)
    start_positions = [offset for offset in range(1 - WIN, WIN) if offset != 0]
    selectors = {}
    for offset in start_positions:
        matching = pool_owner == dom_index + offset
        selectors[offset] = (slot_rank[None, :] == cap_index[:, None]) & matching[None, :]
    arrivals = {}
    for offset in start_positions:
        sel = selectors[offset]
        arrivals[offset] = passed_along(
            (
                select_rows(sel, flat_pooled),
                jnp.sum(jnp.where(sel, slot_index[None, :] + 1, 0), axis=1),
            ),
            "dom",
            offset,
        )
    mine = (pool_owner == dom_index)[:, None, None]
    coarse_total = (
        jnp.where(mine, pooled, jnp.zeros_like(pooled)).astype(jnp.float32).reshape(block_count, -1)
    )
    placings = {}
    for offset in start_positions:
        arrived_tiles, arrived_tags = arrivals[offset]
        placing = arrived_tags[None, :] == slot_index[:, None] + 1
        placings[offset] = placing
        coarse_total = coarse_total + jnp.dot(
            placing.astype(jnp.bfloat16), arrived_tiles, preferred_element_type=jnp.float32
        )
    pooled_level_vectors = block_count * tile_rows
    coarse = coarse_total.astype(jnp.bfloat16).reshape(pooled_level_vectors, feature_width)
    partial_graph_number = lax.axis_size("sub")
    own_sub = lax.axis_index("sub")
    source_sub = (own_sub + pooled_block_source_index) % partial_graph_number
    source_onehot = (
        source_sub[:, None] == jnp.arange(partial_graph_number, dtype=jnp.int32)[None, :]
    ).astype(jnp.float32)
    merged_features = jnp.einsum(
        "kj,krc->rjc",
        source_onehot,
        coarse_tiles.astype(jnp.float32),
        precision=lax.Precision.HIGHEST,
    )
    merged_features = merged_features.reshape(
        pooled_level_vectors, partial_graph_number * pooled_level_vectors
    )
    coarse_message_rows = jnp.dot(
        merged_features,
        lax.all_gather(coarse, "sub", axis=0, tiled=True).astype(jnp.float32),
        precision=lax.Precision.HIGHEST,
    )
    coarse_message_rows = coarse_message_rows.astype(jnp.bfloat16)
    coarse_delta = node_update(
        coarse,
        coarse_message_rows,
        coarse_first,
        coarse_bias,
        coarse_second,
        pooled_level_scale_factor,
    )
    coarse_delta = coarse_delta.astype(jnp.bfloat16).reshape(block_count, tile_rows, feature_width)
    halo_count = halo_blocks.shape[0] // 2
    chosen = blocks[halo_blocks]
    from_lower = passed_along(chosen[halo_count:], ("dom", "sub"), 1)
    from_upper = passed_along(chosen[:halo_count], ("dom", "sub"), -1)
    sender_index_matrix = jnp.concatenate([blocks, from_lower, from_upper], axis=0)
    gathered = sender_index_matrix[edge_source]
    products = jnp.einsum("ers,esd->erd", edge_tiles, gathered, preferred_element_type=jnp.float32)
    entry_count = edge_tiles.shape[0]
    live_mask = (jnp.arange(entry_count, dtype=jnp.int32) < edge_count[0]).astype(jnp.float32)
    target_onehot = (edge_target[:, None] == slot_index[None, :]).astype(jnp.float32) * live_mask[
        :, None
    ]
    messages = jnp.einsum("eb,erd->brd", target_onehot, products, precision=lax.Precision.HIGHEST)
    messages = messages.astype(jnp.bfloat16).reshape(block_count * block_rows, feature_width)
    fine_delta = node_update(fine_nodes, messages, fine_first, fine_bias, fine_second, fine_gain)
    flattened_update = coarse_delta.reshape(block_count, -1)
    replies = {}
    for offset in start_positions:
        replies[offset] = select_rows(placings[offset].T, flattened_update)
    back_total = (
        jnp.where(mine, coarse_delta, jnp.zeros_like(coarse_delta))
        .astype(jnp.float32)
        .reshape(block_count, -1)
    )
    for offset in start_positions:
        incoming_rows = passed_along(replies[offset], "dom", -offset)
        back_total = back_total + jnp.dot(
            selectors[offset].T.astype(jnp.bfloat16),
            incoming_rows,
            preferred_element_type=jnp.float32,
        )
    back = back_total.astype(jnp.bfloat16).reshape(block_count, tile_rows, feature_width)
    unpooled = jnp.repeat(back, POOL, axis=1).reshape(block_count * block_rows, feature_width)
    fine_out = fine_nodes.astype(jnp.float32) + fine_delta + unpooled.astype(jnp.float32)
    return fine_out.astype(jnp.bfloat16)


def solution(mesh):
    placed = (
        P(("dom", "sub"), None),
        P(("dom", "sub"), None, None),
        P(("dom", "sub")),
        P(("dom", "sub")),
        P(("dom", "sub")),
        P(("dom", "sub")),
        P(("dom", "sub")),
        P(("dom", "sub"), None, None),
        P(("dom", "sub")),
        P(),
        P(),
        P(),
        P(),
        P(),
        P(),
        P(),
        P(),
    )
    return jax.shard_map(
        per_device, mesh=mesh, in_specs=placed, out_specs=P(("dom", "sub"), None), check_vma=False
    )
```

profile of v0, /device:TPU:32, one launch (start us, length us, event | category | flops | bytes accessed | tf_op | source)
XLA Modules:
  0.0 184.2 jit_solution(11379934443305981202)
XLA Ops:
  2.9 4.3 %collective-permute-start.10 = (s32[2]{0:T(128)S(1)}, s32[2]{0:T(128)S(1)}, u32[]{:S(2)}, u32[]{:S(2)}) collective-permute-start(s32[2]{0:T(128)S(1)} %get-tuple-element.9), channel_id=1, source_target_pairs={{0,8},{4,12},{8,16},{12,20},{16,24},{20,28},{24,32},{28,36},{32,40... | collective-permute-start | bytes 32 | tf_op jit(solution)/shard_map/ppermute | solution.py:13
  12.9 4.3 %collective-permute-start.11 = (bf16[2,8192]{1,0:T(2,128)(2,1)S(1)}, bf16[2,8192]{1,0:T(2,128)(2,1)S(1)}, u32[]{:S(2)}, u32[]{:S(2)}) collective-permute-start(bf16[2,8192]{1,0:T(2,128)(2,1)S(1)} %convolution_convert_fusion.7), channel_id=1, source_target_pairs={{0,8},{4,12},{8,16},{12,20},{16,24},{20,28},{24,32},{28,36},{32,40... | collective-permute-start | bytes 98312 | tf_op jit(solution)/shard_map/ppermute | solution.py:13
  19.3 4.4 %collective-permute-start.9 = (bf16[2,8192]{1,0:T(2,128)(2,1)S(1)}, bf16[2,8192]{1,0:T(2,128)(2,1)S(1)}, u32[]{:S(2)}, u32[]{:S(2)}) collective-permute-start(bf16[2,8192]{1,0:T(2,128)(2,1)S(1)} %convolution_convert_fusion.8), channel_id=1, source_target_pairs={{0,4},{4,8},{8,12},{12,16},{16,20},{20,24},{24,28},{28,32},{32,36}... | collective-permute-start | bytes 98312 | tf_op jit(solution)/shard_map/ppermute | solution.py:13
  23.7 4.5 %collective-permute-start.6 = (s32[2]{0:T(128)S(1)}, s32[2]{0:T(128)S(1)}, u32[]{:S(2)}, u32[]{:S(2)}) collective-permute-start(s32[2]{0:T(128)S(1)} %get-tuple-element.7), channel_id=1, source_target_pairs={{4,0},{8,4},{12,8},{16,12},{20,16},{24,20},{28,24},{32,28},{36,32}... | collective-permute-start | bytes 32 | tf_op jit(solution)/shard_map/ppermute | solution.py:13
  35.5 2.4 %collective-permute-start.7 = (bf16[2,8192]{1,0:T(2,128)(2,1)S(1)}, bf16[2,8192]{1,0:T(2,128)(2,1)S(1)}, u32[]{:S(2)}, u32[]{:S(2)}) collective-permute-start(bf16[2,8192]{1,0:T(2,128)(2,1)S(1)} %convolution_convert_fusion.9), channel_id=1, source_target_pairs={{4,0},{8,4},{12,8},{16,12},{20,16},{24,20},{28,24},{32,28},{36,32}... | collective-permute-start | bytes 98312 | tf_op jit(solution)/shard_map/ppermute | solution.py:13
  37.9 2.8 %collective-permute-start.4 = (s32[2]{0:T(128)}, s32[2]{0:T(128)S(1)}, u32[]{:S(2)}, u32[]{:S(2)}) collective-permute-start(s32[2]{0:T(128)} %get-tuple-element.6), channel_id=1, source_target_pairs={{8,0},{12,4},{16,8},{20,12},{24,16},{28,20},{32,24},{36,28},{40,32... | collective-permute-start | bytes 32 | tf_op jit(solution)/shard_map/ppermute | solution.py:13
  41.0 3.9 %collective-permute-start.5 = (bf16[2,8192]{1,0:T(2,128)(2,1)}, bf16[2,8192]{1,0:T(2,128)(2,1)S(1)}, u32[]{:S(2)}, u32[]{:S(2)}) collective-permute-start(bf16[2,8192]{1,0:T(2,128)(2,1)} %convolution_convert_fusion.10), channel_id=1, source_target_pairs={{8,0},{12,4},{16,8},{20,12},{24,16},{28,20},{32,24},{36,28},{40,32... | collective-permute-start | bytes 98312 | tf_op jit(solution)/shard_map/ppermute | solution.py:13
  47.1 2.8 %collective-permute-start.13 = (bf16[2,8192]{1,0:T(2,128)(2,1)}, bf16[2,8192]{1,0:T(2,128)(2,1)S(1)}, u32[]{:S(2)}, u32[]{:S(2)}) collective-permute-start(bf16[2,8192]{1,0:T(2,128)(2,1)} %convolution_convert_fusion.6), channel_id=1, source_target_pairs={{0,12},{4,16},{8,20},{12,24},{16,28},{20,32},{24,36},{28,40},{32,4... | collective-permute-start | bytes 98312 | tf_op jit(solution)/shard_map/ppermute | solution.py:13
  50.0 7.1 %collective-permute-start.2 = (s32[2]{0:T(128)}, s32[2]{0:T(128)S(1)}, u32[]{:S(2)}, u32[]{:S(2)}) collective-permute-start(s32[2]{0:T(128)} %get-tuple-element.5), channel_id=1, source_target_pairs={{12,0},{16,4},{20,8},{24,12},{28,16},{32,20},{36,24},{40,28},{44,3... | collective-permute-start | bytes 32 | tf_op jit(solution)/shard_map/ppermute | solution.py:13
  58.0 3.6 %collective-permute-start.3 = (bf16[2,8192]{1,0:T(2,128)(2,1)S(1)}, bf16[2,8192]{1,0:T(2,128)(2,1)S(1)}, u32[]{:S(2)}, u32[]{:S(2)}) collective-permute-start(bf16[2,8192]{1,0:T(2,128)(2,1)S(1)} %copy-done.6), channel_id=1, source_target_pairs={{12,0},{16,4},{20,8},{24,12},{28,16},{32,20},{36,24},{40,28},{44,3... | collective-permute-start | bytes 98312 | tf_op jit(solution)/shard_map/ppermute | solution.py:13
  61.6 3.4 %collective-permute-start = (bf16[2,128,512]{2,1,0:T(8,128)(2,1)}, bf16[2,128,512]{2,1,0:T(8,128)(2,1)}, u32[]{:S(2)}, u32[]{:S(2)}) collective-permute-start(bf16[2,128,512]{2,1,0:T(8,128)(2,1)} %get-tuple-element.11), channel_id=1, source_target_pairs={{0,1},{1,2},{2,3},{3,4},{4,5},{5,6},{6,7},{7,8},{8,9},{9,10},{10,1... | collective-permute-start | bytes 786440 | tf_op jit(solution)/shard_map/ppermute | solution.py:13
  65.3 7.6 %collective-permute-start.1 = (bf16[2,128,512]{2,1,0:T(8,128)(2,1)}, bf16[2,128,512]{2,1,0:T(8,128)(2,1)}, u32[]{:S(2)}, u32[]{:S(2)}) collective-permute-start(bf16[2,128,512]{2,1,0:T(8,128)(2,1)} %get-tuple-element.12), channel_id=1, source_target_pairs={{1,0},{2,1},{3,2},{4,3},{5,4},{6,5},{7,6},{8,7},{9,8},{10,9},{11,1... | collective-permute-start | bytes 786440 | tf_op jit(solution)/shard_map/ppermute | solution.py:13
  76.3 13.2 %all_gather.3 = bf16[512,512]{1,0:T(8,128)(2,1)S(1)} all-gather(bf16[128,512]{1,0:T(8,128)(2,1)S(1)} %reshape.95), channel_id=1, replica_groups=mesh['dom'=128,'sub'=4] {'sub'}, dimensions={0}, use_global_device_ids=true | all-gather | bytes 655360 | tf_op jit(solution)/shard_map/all_gather | solution.py:122
  99.4 7.0 %collective-permute-start.17 = (bf16[2,8192]{1,0:T(2,128)(2,1)S(1)}, bf16[2,8192]{1,0:T(2,128)(2,1)S(1)}, u32[]{:S(2)}, u32[]{:S(2)}) collective-permute-start(bf16[2,8192]{1,0:T(2,128)(2,1)S(1)} %convolution_convert_fusion.2), channel_id=1, source_target_pairs={{4,0},{8,4},{12,8},{16,12},{20,16},{24,20},{28,24},{32,28},{36,32}... | collective-permute-start | bytes 98312 | tf_op jit(solution)/shard_map/ppermute | solution.py:13
  107.3 3.9 %collective-permute-start.18 = (bf16[2,8192]{1,0:T(2,128)(2,1)S(1)}, bf16[2,8192]{1,0:T(2,128)(2,1)S(1)}, u32[]{:S(2)}, u32[]{:S(2)}) collective-permute-start(bf16[2,8192]{1,0:T(2,128)(2,1)S(1)} %convolution_convert_fusion.1), channel_id=1, source_target_pairs={{8,0},{12,4},{16,8},{20,12},{24,16},{28,20},{32,24},{36,28},{40,32... | collective-permute-start | bytes 98312 | tf_op jit(solution)/shard_map/ppermute | solution.py:13
  113.7 3.8 %collective-permute-start.14 = (bf16[2,8192]{1,0:T(2,128)(2,1)S(1)}, bf16[2,8192]{1,0:T(2,128)(2,1)S(1)}, u32[]{:S(2)}, u32[]{:S(2)}) collective-permute-start(bf16[2,8192]{1,0:T(2,128)(2,1)S(1)} %convolution_convert_fusion.5), channel_id=1, source_target_pairs={{0,12},{4,16},{8,20},{12,24},{16,28},{20,32},{24,36},{28,40},{32,4... | collective-permute-start | bytes 98312 | tf_op jit(solution)/shard_map/ppermute | solution.py:13
  118.2 5.0 %collective-permute-done.14 = bf16[2,8192]{1,0:T(2,128)(2,1)S(1)} collective-permute-done((bf16[2,8192]{1,0:T(2,128)(2,1)S(1)}, bf16[2,8192]{1,0:T(2,128)(2,1)S(1)}, u32[]{:S(2)}, u32[]{:S(2)}) %collective-permute-start.14) | collective-permute-done | bytes 32800 | tf_op jit(solution)/shard_map/ppermute | solution.py:13
  125.1 2.9 %copy.53 = f32[1024,512]{0,1:T(8,128)} copy(f32[1024,512]{1,0:T(8,128)} %bitcast.64) | data formatting | bytes 4194304 | tf_op jit(solution)/shard_map/convert_element_type | solution.py:168
  129.6 5.3 %gather_fusion.1 = bf16[56,128,512]{2,1,0:T(8,128)(2,1)} fusion(bf16[12,128,512]{2,1,0:T(8,128)(2,1)S(1)} %pad_maximum_fusion, s32[1024]{0:T(1024)} %pad_clamp_fusion), kind=kCustom, calls=%fused_computation.1 | custom fusion | bytes 14680288 | tf_op jit(solution)/shard_map/gather | solution.py:140
  135.0 10.4 %convolution_bitcast_fusion = f32[56,128,512]{1,2,0:T(8,128)} fusion(bf16[56,128,512]{2,1,0:T(8,128)(2,1)} %gather_fusion.1, bf16[56,128,128]{2,1,0:T(8,128)(2,1)S(1)} %copy-done), kind=kOutput, calls=%fused_computation.28 | convolution fusion | flops 939524096 | bytes 23855104 | tf_op jit(solution)/shard_map/ers,esd->erd/dot_general | solution.py:141
  145.4 16.4 %copy.48 = f32[56,128,512]{2,0,1:T(8,128)} copy(f32[56,128,512]{1,2,0:T(8,128)} %convolution_bitcast_fusion) | data formatting | bytes 29360128 | tf_op jit(solution)/shard_map/ers,esd->erd/dot_general | solution.py:141
  161.9 10.0 %convolution_convert_fusion.12 = bf16[8,128,512]{2,0,1:T(8,128)(2,1)S(1)} fusion(f32[56,128,512]{2,0,1:T(8,128)} %copy.48, f32[56]{0:T(128)S(1)} %copy-done.28, s32[56]{0:T(128)S(1)} %copy-done.27), kind=kOutput, calls=%fused_computation.38 | convolution fusion | flops 352846720 | bytes 15729088 | tf_op jit(solution)/shard_map/eb,erd->brd/dot_general | solution.py:147
  173.5 4.7 %fusion.125 = (f32[1024]{0:T(1024)S(1)}, f32[1024,512]{0,1:T(8,128)}) fusion(bf16[512,512]{1,0:T(8,128)(2,1)S(1)} %copy-done.29, bf16[1024,512]{1,0:T(8,128)(2,1)} %param.26, bf16[1024,512]{1,0:T(8,128)(2,1)} %bitcast.68, bf16[1024,512]{1,0:T(8,128)(2,1)S(1)} %copy-done.3, f32[512]{0:T(512)S(1)} %copy-done.30), kind=kOutput, calls=%fused_computation.160 | convolution fusion | flops 1616903168 | bytes 5773312 | tf_op jit(solution)/shard_map/dot_general | solution.py:29
  180.1 2.7 %add_convert_fusion = bf16[1024,512]{0,1:T(8,128)(2,1)S(1)} fusion(f32[1024,512]{0,1:T(8,128)} %copy.53, f32[1024,512]{0,1:T(8,128)} %get-tuple-element.23, f32[512]{0:T(512)S(1)} %copy-done.18, f32[1024]{0:T(1024)S(1)} %add_rsqrt_fusion, f32[1024]{0:T(1024)S(1)} %broadcast_multiply_fusion, bf16[1024,512]{0,1:T(8,128)(2,1)S(1)} %copy-done.2), kind=kLoop, calls=%fused_computation.34 | loop fusion | flops 3670016 | bytes 6301696 | tf_op jit(solution)/shard_map/convert_element_type | solution.py:169
  (150 shorter events, 46.2 us)
Async XLA Ops:
  0.0 135.0 %copy-start = (bf16[56,128,128]{2,1,0:T(8,128)(2,1)S(1)}, bf16[56,128,128]{2,1,0:T(8,128)(2,1)}, u32[]{:S(2)}) copy-start(bf16[56,128,128]{2,1,0:T(8,128)(2,1)} %param.18) | copy-start | bytes 5505028
  2.9 32.5 %collective-permute-start.10 = (s32[2]{0:T(128)S(1)}, s32[2]{0:T(128)S(1)}, u32[]{:S(2)}, u32[]{:S(2)}) collective-permute-start(s32[2]{0:T(128)S(1)} %get-tuple-element.9), channel_id=1, source_target_pairs={{0,8},{4,12},{8,16},{12,20},{16,24},{20,28},{24,32},{28,36},{32,40... | collective-permute-start | bytes 32 | tf_op jit(solution)/shard_map/ppermute | solution.py:13
  12.9 25.0 %collective-permute-start.11 = (bf16[2,8192]{1,0:T(2,128)(2,1)S(1)}, bf16[2,8192]{1,0:T(2,128)(2,1)S(1)}, u32[]{:S(2)}, u32[]{:S(2)}) collective-permute-start(bf16[2,8192]{1,0:T(2,128)(2,1)S(1)} %convolution_convert_fusion.7), channel_id=1, source_target_pairs={{0,8},{4,12},{8,16},{12,20},{16,24},{20,28},{24,32},{28,36},{32,40... | collective-permute-start | bytes 98312 | tf_op jit(solution)/shard_map/ppermute | solution.py:13
  17.2 23.7 %collective-permute-start.8 = (s32[2]{0:T(128)S(1)}, s32[2]{0:T(128)S(1)}, u32[]{:S(2)}, u32[]{:S(2)}) collective-permute-start(s32[2]{0:T(128)S(1)} %get-tuple-element.8), channel_id=1, source_target_pairs={{0,4},{4,8},{8,12},{12,16},{16,20},{20,24},{24,28},{28,32},{32,36}... | collective-permute-start | bytes 32 | tf_op jit(solution)/shard_map/ppermute | solution.py:13
  19.3 25.6 %collective-permute-start.9 = (bf16[2,8192]{1,0:T(2,128)(2,1)S(1)}, bf16[2,8192]{1,0:T(2,128)(2,1)S(1)}, u32[]{:S(2)}, u32[]{:S(2)}) collective-permute-start(bf16[2,8192]{1,0:T(2,128)(2,1)S(1)} %convolution_convert_fusion.8), channel_id=1, source_target_pairs={{0,4},{4,8},{8,12},{12,16},{16,20},{20,24},{24,28},{28,32},{32,36}... | collective-permute-start | bytes 98312 | tf_op jit(solution)/shard_map/ppermute | solution.py:13
  23.7 23.3 %collective-permute-start.6 = (s32[2]{0:T(128)S(1)}, s32[2]{0:T(128)S(1)}, u32[]{:S(2)}, u32[]{:S(2)}) collective-permute-start(s32[2]{0:T(128)S(1)} %get-tuple-element.7), channel_id=1, source_target_pairs={{4,0},{8,4},{12,8},{16,12},{20,16},{24,20},{28,24},{32,28},{36,32}... | collective-permute-start | bytes 32 | tf_op jit(solution)/shard_map/ppermute | solution.py:13
  35.5 14.4 %collective-permute-start.7 = (bf16[2,8192]{1,0:T(2,128)(2,1)S(1)}, bf16[2,8192]{1,0:T(2,128)(2,1)S(1)}, u32[]{:S(2)}, u32[]{:S(2)}) collective-permute-start(bf16[2,8192]{1,0:T(2,128)(2,1)S(1)} %convolution_convert_fusion.9), channel_id=1, source_target_pairs={{4,0},{8,4},{12,8},{16,12},{20,16},{24,20},{28,24},{32,28},{36,32}... | collective-permute-start | bytes 98312 | tf_op jit(solution)/shard_map/ppermute | solution.py:13
  37.9 20.1 %collective-permute-start.4 = (s32[2]{0:T(128)}, s32[2]{0:T(128)S(1)}, u32[]{:S(2)}, u32[]{:S(2)}) collective-permute-start(s32[2]{0:T(128)} %get-tuple-element.6), channel_id=1, source_target_pairs={{8,0},{12,4},{16,8},{20,12},{24,16},{28,20},{32,24},{36,28},{40,32... | collective-permute-start | bytes 32 | tf_op jit(solution)/shard_map/ppermute | solution.py:13
  41.0 20.7 %collective-permute-start.5 = (bf16[2,8192]{1,0:T(2,128)(2,1)}, bf16[2,8192]{1,0:T(2,128)(2,1)S(1)}, u32[]{:S(2)}, u32[]{:S(2)}) collective-permute-start(bf16[2,8192]{1,0:T(2,128)(2,1)} %convolution_convert_fusion.10), channel_id=1, source_target_pairs={{8,0},{12,4},{16,8},{20,12},{24,16},{28,20},{32,24},{36,28},{40,32... | collective-permute-start | bytes 98312 | tf_op jit(solution)/shard_map/ppermute | solution.py:13
  44.9 20.4 %collective-permute-start.12 = (s32[2]{0:T(128)}, s32[2]{0:T(128)S(1)}, u32[]{:S(2)}, u32[]{:S(2)}) collective-permute-start(s32[2]{0:T(128)} %get-tuple-element.10), channel_id=1, source_target_pairs={{0,12},{4,16},{8,20},{12,24},{16,28},{20,32},{24,36},{28,40},{32,4... | collective-permute-start | bytes 32 | tf_op jit(solution)/shard_map/ppermute | solution.py:13
  47.1 25.8 %collective-permute-start.13 = (bf16[2,8192]{1,0:T(2,128)(2,1)}, bf16[2,8192]{1,0:T(2,128)(2,1)S(1)}, u32[]{:S(2)}, u32[]{:S(2)}) collective-permute-start(bf16[2,8192]{1,0:T(2,128)(2,1)} %convolution_convert_fusion.6), channel_id=1, source_target_pairs={{0,12},{4,16},{8,20},{12,24},{16,28},{20,32},{24,36},{28,40},{32,4... | collective-permute-start | bytes 98312 | tf_op jit(solution)/shard_map/ppermute | solution.py:13
  49.9 40.6 %copy-start.4 = (bf16[1024,512]{1,0:T(8,128)(2,1)S(1)}, bf16[1024,512]{1,0:T(8,128)(2,1)}, u32[]{:S(2)}) copy-start(bf16[1024,512]{1,0:T(8,128)(2,1)} %param.30) | copy-start | bytes 3145732
  50.0 23.2 %collective-permute-start.2 = (s32[2]{0:T(128)}, s32[2]{0:T(128)S(1)}, u32[]{:S(2)}, u32[]{:S(2)}) collective-permute-start(s32[2]{0:T(128)} %get-tuple-element.5), channel_id=1, source_target_pairs={{12,0},{16,4},{20,8},{24,12},{28,16},{32,20},{36,24},{40,28},{44,3... | collective-permute-start | bytes 32 | tf_op jit(solution)/shard_map/ppermute | solution.py:13
  58.0 15.2 %collective-permute-start.3 = (bf16[2,8192]{1,0:T(2,128)(2,1)S(1)}, bf16[2,8192]{1,0:T(2,128)(2,1)S(1)}, u32[]{:S(2)}, u32[]{:S(2)}) collective-permute-start(bf16[2,8192]{1,0:T(2,128)(2,1)S(1)} %copy-done.6), channel_id=1, source_target_pairs={{12,0},{16,4},{20,8},{24,12},{28,16},{32,20},{36,24},{40,28},{44,3... | collective-permute-start | bytes 98312 | tf_op jit(solution)/shard_map/ppermute | solution.py:13
  61.6 66.4 %collective-permute-start = (bf16[2,128,512]{2,1,0:T(8,128)(2,1)}, bf16[2,128,512]{2,1,0:T(8,128)(2,1)}, u32[]{:S(2)}, u32[]{:S(2)}) collective-permute-start(bf16[2,128,512]{2,1,0:T(8,128)(2,1)} %get-tuple-element.11), channel_id=1, source_target_pairs={{0,1},{1,2},{2,3},{3,4},{4,5},{5,6},{6,7},{7,8},{8,9},{9,10},{10,1... | collective-permute-start | bytes 786440 | tf_op jit(solution)/shard_map/ppermute | solution.py:13
  65.3 62.8 %collective-permute-start.1 = (bf16[2,128,512]{2,1,0:T(8,128)(2,1)}, bf16[2,128,512]{2,1,0:T(8,128)(2,1)}, u32[]{:S(2)}, u32[]{:S(2)}) collective-permute-start(bf16[2,128,512]{2,1,0:T(8,128)(2,1)} %get-tuple-element.12), channel_id=1, source_target_pairs={{1,0},{2,1},{3,2},{4,3},{5,4},{6,5},{7,6},{8,7},{9,8},{10,9},{11,1... | collective-permute-start | bytes 786440 | tf_op jit(solution)/shard_map/ppermute | solution.py:13
  90.5 27.2 %copy-start.8 = (pred[8]{0:T(512)(128)(4,1)S(1)}, pred[8]{0:T(512)(128)(4,1)}, u32[]{:S(2)}) copy-start(pred[8]{0:T(512)(128)(4,1)} %copy-done.7) | copy-start | bytes 28
  92.3 31.0 %copy-start.15 = (pred[8]{0:T(512)(128)(4,1)S(1)}, pred[8]{0:T(512)(128)(4,1)}, u32[]{:S(2)}) copy-start(pred[8]{0:T(512)(128)(4,1)} %get-tuple-element.13) | copy-start | bytes 28
  94.2 13.0 %collective-permute-start.15 = (bf16[2,8192]{1,0:T(2,128)(2,1)S(1)}, bf16[2,8192]{1,0:T(2,128)(2,1)S(1)}, u32[]{:S(2)}, u32[]{:S(2)}) collective-permute-start(bf16[2,8192]{1,0:T(2,128)(2,1)S(1)} %convolution_convert_fusion.4), channel_id=1, source_target_pairs={{0,8},{4,12},{8,16},{12,20},{16,24},{20,28},{24,32},{28,36},{32,40... | collective-permute-start | bytes 98312 | tf_op jit(solution)/shard_map/ppermute | solution.py:13
  97.1 14.3 %collective-permute-start.16 = (bf16[2,8192]{1,0:T(2,128)(2,1)S(1)}, bf16[2,8192]{1,0:T(2,128)(2,1)S(1)}, u32[]{:S(2)}, u32[]{:S(2)}) collective-permute-start(bf16[2,8192]{1,0:T(2,128)(2,1)S(1)} %convolution_convert_fusion.3), channel_id=1, source_target_pairs={{0,4},{4,8},{8,12},{12,16},{16,20},{20,24},{24,28},{28,32},{32,36}... | collective-permute-start | bytes 98312 | tf_op jit(solution)/shard_map/ppermute | solution.py:13
  99.4 14.3 %collective-permute-start.17 = (bf16[2,8192]{1,0:T(2,128)(2,1)S(1)}, bf16[2,8192]{1,0:T(2,128)(2,1)S(1)}, u32[]{:S(2)}, u32[]{:S(2)}) collective-permute-start(bf16[2,8192]{1,0:T(2,128)(2,1)S(1)} %convolution_convert_fusion.2), channel_id=1, source_target_pairs={{4,0},{8,4},{12,8},{16,12},{20,16},{24,20},{28,24},{32,28},{36,32}... | collective-permute-start | bytes 98312 | tf_op jit(solution)/shard_map/ppermute | solution.py:13
  107.3 10.4 %collective-permute-start.18 = (bf16[2,8192]{1,0:T(2,128)(2,1)S(1)}, bf16[2,8192]{1,0:T(2,128)(2,1)S(1)}, u32[]{:S(2)}, u32[]{:S(2)}) collective-permute-start(bf16[2,8192]{1,0:T(2,128)(2,1)S(1)} %convolution_convert_fusion.1), channel_id=1, source_target_pairs={{8,0},{12,4},{16,8},{20,12},{24,16},{28,20},{32,24},{36,28},{40,32... | collective-permute-start | bytes 98312 | tf_op jit(solution)/shard_map/ppermute | solution.py:13
  111.5 6.5 %collective-permute-start.19 = (bf16[2,8192]{1,0:T(2,128)(2,1)S(1)}, bf16[2,8192]{1,0:T(2,128)(2,1)S(1)}, u32[]{:S(2)}, u32[]{:S(2)}) collective-permute-start(bf16[2,8192]{1,0:T(2,128)(2,1)S(1)} %convolution_convert_fusion), channel_id=1, source_target_pairs={{12,0},{16,4},{20,8},{24,12},{28,16},{32,20},{36,24},{40,28},{44,3... | collective-permute-start | bytes 98312 | tf_op jit(solution)/shard_map/ppermute | solution.py:13
  113.7 9.6 %collective-permute-start.14 = (bf16[2,8192]{1,0:T(2,128)(2,1)S(1)}, bf16[2,8192]{1,0:T(2,128)(2,1)S(1)}, u32[]{:S(2)}, u32[]{:S(2)}) collective-permute-start(bf16[2,8192]{1,0:T(2,128)(2,1)S(1)} %convolution_convert_fusion.5), channel_id=1, source_target_pairs={{0,12},{4,16},{8,20},{12,24},{16,28},{20,32},{24,36},{28,40},{32,4... | collective-permute-start | bytes 98312 | tf_op jit(solution)/shard_map/ppermute | solution.py:13
  (30 other events, 412.7 us)
where the time goes:
time: 185 us; the launch traced here: 184 us
  starting transfers between devices  75.4 us (41%)
  matrix products  38.7 us (21%)
  local copies, waits for them, and re-layouts  36.8 us (20%)
  other arithmetic  13.5 us (7%)
  blocking collectives  13.2 us (7%)
  waiting for transfers between devices  5.02 us (3%)
    ppermute x20, starting transfers between devices, passed_along(): return lax.ppermute(block, axis, route)  75.4 us
    dot_general x1, local copies, waits for them, and re-layouts, per_device(): jnp.einsum('ers,esd->erd', edge_tiles, gathered, preferred_element_type=j...  16.4 us
    all_gather x1, blocking collectives, per_device(): lax.all_gather(coarse, 'sub', axis=0, tiled=True).astype(jnp.float32)  13.2 us
    dot_general x1, matrix products, per_device(): jnp.einsum('ers,esd->erd', edge_tiles, gathered, preferred_element_type=j...  10.4 us
    dot_general x1, matrix products, per_device(): jnp.einsum('eb,erd->brd', target_onehot, products, precision=lax.Precisio...  9.96 us
    dot_general x2, matrix products, node_update(): jnp.dot(hidden_act, weight_out, preferred_element_type=jnp.float32)  6.34 us
    dot_general x12, matrix products, select_rows(): jnp.dot(selector.astype(jnp.bfloat16), values, preferred_element_type=jnp...  5.82 us
    gather x1, local copies, waits for them, and re-layouts, per_device(): gathered = sender_index_matrix[edge_source]  5.35 us
  transfers between devices with their start and end apart: 20, of which 1 were waited for; matrix products, arithmetic and copies ran while one was open for 16% of the time, Pallas kernels for 0%

commit v1 on v0

v1 whole, which is shorter than its diff:
```python
import functools

import jax
import jax.numpy as jnp
from jax import lax
from jax.experimental import pallas as pl
from jax.experimental.pallas import tpu as pltpu
from jax.sharding import Mesh
from jax.sharding import PartitionSpec as P

POOL = 8
WIN = 4
GROUP = 4
F32 = jnp.float32
BF16 = jnp.bfloat16

VMEM_SPEC = pl.BlockSpec(memory_space=pltpu.VMEM)
SMEM_SPEC = pl.BlockSpec(memory_space=pltpu.SMEM)
ANY_SPEC = pl.BlockSpec(memory_space=pl.ANY)


def owner_slots(owner_ref, count_ref, block_count):
    for d in range(WIN):
        count_ref[d] = 0
    slots = []
    for k in range(block_count):
        d = owner_ref[k] & (WIN - 1)
        r = count_ref[d]
        count_ref[d] = r + 1
        slots.append((d, r))
    return slots


def pack_kernel(owner_ref, halo_ref, nodes_ref, send_ref, lower_ref, upper_ref, count_ref, index_ref):
    blocks, rows, width = nodes_ref.shape
    tile = rows // POOL
    lanes = send_ref.shape[-1]
    groups = width // lanes
    subs = send_ref.shape[0] // WIN
    halo = halo_ref.shape[0] // 2
    for h in range(halo):
        lower_ref[h] = nodes_ref[halo_ref[h]]
        upper_ref[h] = nodes_ref[halo_ref[halo + h]]
    row = lax.broadcasted_iota(jnp.int32, (tile, rows), 0)
    col = lax.broadcasted_iota(jnp.int32, (tile, rows), 1)
    average = jnp.where(col // POOL == row, 1.0 / POOL, 0.0).astype(BF16)
    for k, (d, r) in enumerate(owner_slots(owner_ref, count_ref, blocks)):
        index_ref[d * 2 + r] = k
        pooled = jnp.dot(average, nodes_ref[k], preferred_element_type=F32).astype(BF16)
        for s in range(subs):
            for c in range(groups):
                send_ref[d * subs + s, c * 2 + r] = pooled[:, c * lanes : (c + 1) * lanes]
    lane = lax.broadcasted_iota(jnp.int32, (tile, lanes), 1)
    for d in range(WIN):
        tag = jnp.where((lane // tile) % 2 == 0, index_ref[2 * d], index_ref[2 * d + 1])
        tag = tag.astype(F32).astype(BF16)
        for s in range(subs):
            send_ref[d * subs + s, groups * 2] = tag


def pack(pool_owner, halo_blocks, blocks, subs):
    count, rows, width = blocks.shape
    tile = rows // POOL
    halo = halo_blocks.shape[0] // 2
    lanes = 128
    return pl.pallas_call(
        pack_kernel,
        name="pack",
        out_shape=(
            jax.ShapeDtypeStruct((WIN * subs, 2 * (width // lanes) + 1, tile, lanes), BF16),
            jax.ShapeDtypeStruct((halo, rows, width), BF16),
            jax.ShapeDtypeStruct((halo, rows, width), BF16),
        ),
        in_specs=[SMEM_SPEC, SMEM_SPEC, VMEM_SPEC],
        out_specs=(VMEM_SPEC,) * 3,
        scratch_shapes=[pltpu.SMEM((WIN,), jnp.int32), pltpu.SMEM((2 * WIN,), jnp.int32)],
        compiler_params=pltpu.CompilerParams(vmem_limit_bytes=16 << 20),
        cost_estimate=pl.CostEstimate(flops=1 << 27, bytes_accessed=3 << 20, transcendentals=0),
    )(pool_owner, halo_blocks, blocks)


def normalised(values, gain):
    row_mean = jnp.mean(values, axis=-1, keepdims=True)
    centred = values - row_mean
    variance = jnp.mean(centred * centred, axis=-1, keepdims=True)
    return centred * lax.rsqrt(variance + 1e-05) * gain


def network(nodes, messages, first_ref, bias_ref, second_ref, gain_ref):
    width = nodes.shape[1]
    hidden = jnp.dot(nodes, first_ref[:width], preferred_element_type=F32)
    hidden += jnp.dot(messages, first_ref[width:], preferred_element_type=F32)
    hidden = jnp.maximum(hidden + bias_ref[...], 0.0).astype(BF16)
    projected = jnp.dot(hidden, second_ref[...], preferred_element_type=F32)
    return normalised(projected, gain_ref[...])


def coarse_kernel(sub_ref, arrived_ref, tiles_ref, first_ref, bias_ref, second_ref, gain_ref, reply_ref):
    senders, pieces, tile, lanes = arrived_ref.shape
    groups = pieces // 2
    subs = senders // WIN
    rows = tiles_ref.shape[1]
    row = lax.broadcasted_iota(jnp.int32, (rows, rows), 0)
    col = lax.broadcasted_iota(jnp.int32, (rows, rows), 1)
    same_row = row % tile == col % tile

    def arrived_rows(s):
        return jnp.concatenate(
            [
                jnp.concatenate([arrived_ref[m * subs + s, c * 2 + r] for c in range(groups)], axis=1)
                for m in range(WIN)
                for r in range(2)
            ],
            axis=0,
        )

    def placing(s):
        tags = jnp.zeros((8, lanes), F32)
        lane = lax.broadcasted_iota(jnp.int32, (8, lanes), 1)
        for m in range(WIN):
            tag = arrived_ref[m * subs + s, groups * 2].astype(F32)[:8]
            tags = jnp.where(lane // (2 * tile) == m, tag, tags)
        return jnp.where(same_row & (row // tile == tags[:1].astype(jnp.int32)), 1.0, 0.0)

    own = sub_ref[0]
    own_rows = arrived_rows(own)
    own_back = placing(own).T.astype(BF16)
    weights, sources = [], []
    for e in range(tiles_ref.shape[0]):
        s = sub_ref[1 + e]
        sources.append(arrived_rows(s))
        by_col = jnp.dot(tiles_ref[e], placing(s).astype(BF16), preferred_element_type=F32)
        weights.append(by_col.astype(BF16))
    by_col = jnp.concatenate(weights, axis=1)
    by_both = jnp.dot(own_back, by_col, preferred_element_type=F32).astype(BF16)
    messages = jnp.dot(by_both, jnp.concatenate(sources, axis=0), preferred_element_type=F32)
    delta = network(own_rows, messages.astype(BF16), first_ref, bias_ref, second_ref, gain_ref)
    delta = delta.astype(BF16)
    for m in range(WIN):
        for r in range(2):
            at = (m * 2 + r) * tile
            reply_ref[m, r] = delta[at : at + tile]


def coarse_update(sub_index, arrived, tiles, first, bias, second, gain):
    width = second.shape[0]
    tile = arrived.shape[2]
    return pl.pallas_call(
        coarse_kernel,
        name="coarse",
        out_shape=jax.ShapeDtypeStruct((WIN, 2, tile, width), BF16),
        in_specs=[SMEM_SPEC] + [VMEM_SPEC] * 6,
        out_specs=VMEM_SPEC,
        compiler_params=pltpu.CompilerParams(vmem_limit_bytes=16 << 20),
        cost_estimate=pl.CostEstimate(flops=1 << 29, bytes_accessed=3 << 20, transcendentals=0),
    )(sub_index, arrived, tiles, first, bias, second, gain)


def message_kernel(
    target_ref, source_ref, count_ref, nodes_ref, lower_ref, upper_ref, edges_ref, out_ref,
    table, tiles, total, order_e, order_s, place, sems,
):
    blocks, rows, width = nodes_ref.shape
    entries = edges_ref.shape[0]
    halo = lower_ref.shape[0]
    copies = [
        pltpu.make_async_copy(nodes_ref, table.at[pl.ds(0, blocks)], sems.at[0]),
        pltpu.make_async_copy(edges_ref, tiles.at[pl.ds(0, entries)], sems.at[1]),
        pltpu.make_async_copy(lower_ref, table.at[pl.ds(blocks, halo)], sems.at[2]),
        pltpu.make_async_copy(upper_ref, table.at[pl.ds(blocks + halo, halo)], sems.at[3]),
    ]
    for copy in copies:
        copy.start()
    tiles[entries] = jnp.zeros((rows, rows), BF16)
    live = count_ref[0]

    for b in range(blocks):
        place[b] = 0

    @pl.loop(0, order_e.shape[0])
    def _(i):
        order_e[i] = entries
        order_s[i] = 0

    @pl.loop(0, live)
    def _(e):
        b = target_ref[e]
        place[b] = place[b] + 1

    begins, at = [], 0
    for b in range(blocks):
        steps = (place[b] + (GROUP - 1)) // GROUP
        begins.append((at, steps))
        place[b] = at * GROUP
        at = at + steps

    @pl.loop(0, live)
    def _(e):
        b = target_ref[e]
        at = place[b]
        place[b] = at + 1
        order_e[at] = e
        order_s[at] = source_ref[e]

    for copy in copies:
        copy.wait()
    for b, (begin, steps) in enumerate(begins):
        total[...] = jnp.zeros_like(total)

        @pl.loop(0, steps)
        def _(i):
            at = (begin + i) * GROUP
            left = jnp.concatenate([tiles[order_e[at + g]] for g in range(GROUP)], axis=1)
            right = jnp.concatenate([table[order_s[at + g]] for g in range(GROUP)], axis=0)
            total[...] += jnp.dot(left, right, preferred_element_type=F32)

        out_ref[b] = total[...].astype(BF16)


def block_messages(target, source, count, blocks, lower, upper, edges):
    entries, rows, _ = edges.shape
    block_count, _, width = blocks.shape
    halo = lower.shape[0]
    slots = (entries // GROUP + block_count) * GROUP
    return pl.pallas_call(
        message_kernel,
        name="messages",
        out_shape=jax.ShapeDtypeStruct(blocks.shape, BF16),
        in_specs=[SMEM_SPEC] * 3 + [ANY_SPEC] * 4,
        out_specs=VMEM_SPEC,
        scratch_shapes=[
            pltpu.VMEM((block_count + 2 * halo, rows, width), BF16),
            pltpu.VMEM((entries + 1, rows, rows), BF16),
            pltpu.VMEM((rows, width), F32),
            pltpu.SMEM((slots,), jnp.int32),
            pltpu.SMEM((slots,), jnp.int32),
            pltpu.SMEM((block_count,), jnp.int32),
            pltpu.SemaphoreType.DMA((4,)),
        ],
        compiler_params=pltpu.CompilerParams(vmem_limit_bytes=16 << 20),
        cost_estimate=pl.CostEstimate(flops=1 << 32, bytes_accessed=6 << 20, transcendentals=0),
    )(target, source, count, blocks, lower, upper, edges)


def fine_kernel(nodes_ref, messages_ref, first_ref, bias_ref, second_ref, gain_ref, out_ref):
    step = 256

    @pl.loop(0, nodes_ref.shape[0] // step)
    def _(i):
        at = pl.ds(pl.multiple_of(i * step, step), step)
        nodes = nodes_ref[at]
        delta = network(nodes, messages_ref[at], first_ref, bias_ref, second_ref, gain_ref)
        out_ref[at] = nodes.astype(F32) + delta


def fine_update(nodes, messages, first, bias, second, gain):
    return pl.pallas_call(
        fine_kernel,
        name="fine",
        out_shape=jax.ShapeDtypeStruct(nodes.shape, F32),
        in_specs=[VMEM_SPEC] * 6,
        out_specs=VMEM_SPEC,
        compiler_params=pltpu.CompilerParams(vmem_limit_bytes=16 << 20),
        cost_estimate=pl.CostEstimate(flops=1 << 31, bytes_accessed=6 << 20, transcendentals=0),
    )(nodes, messages, first, bias, second, gain)


def finish_kernel(owner_ref, partial_ref, reply_ref, out_ref, count_ref):
    blocks = owner_ref.shape[0]
    rows = partial_ref.shape[0] // blocks
    tile = rows // POOL
    row = lax.broadcasted_iota(jnp.int32, (rows, tile), 0)
    col = lax.broadcasted_iota(jnp.int32, (rows, tile), 1)
    spread = jnp.where(row // POOL == col, 1.0, 0.0).astype(BF16)
    for k, (d, r) in enumerate(owner_slots(owner_ref, count_ref, blocks)):
        back = jnp.dot(spread, reply_ref[d, r], preferred_element_type=F32)
        at = pl.ds(k * rows, rows)
        out_ref[at] = (partial_ref[at] + back).astype(BF16)


def finish(pool_owner, partial, reply):
    return pl.pallas_call(
        finish_kernel,
        name="finish",
        out_shape=jax.ShapeDtypeStruct(partial.shape, BF16),
        in_specs=[SMEM_SPEC, VMEM_SPEC, VMEM_SPEC],
        out_specs=VMEM_SPEC,
        scratch_shapes=[pltpu.SMEM((WIN,), jnp.int32)],
        compiler_params=pltpu.CompilerParams(vmem_limit_bytes=16 << 20),
        cost_estimate=pl.CostEstimate(flops=1 << 25, bytes_accessed=4 << 20, transcendentals=0),
    )(pool_owner, partial, reply)


def per_device(
    fine_nodes,
    edge_tiles,
    edge_target,
    edge_source,
    edge_count,
    halo_blocks,
    pool_owner,
    coarse_tiles,
    pooled_block_source_index,
    fine_first,
    fine_bias,
    fine_second,
    fine_gain,
    coarse_first,
    coarse_bias,
    coarse_second,
    pooled_level_scale_factor,
):
    block_count = pool_owner.shape[0]
    rows = edge_tiles.shape[1]
    width = fine_nodes.shape[1]
    subs = lax.axis_size("sub")
    everyone = ("win", "mem", "sub")
    devices = lax.axis_size(everyone)
    blocks = fine_nodes.reshape(block_count, rows, width)

    send, lower, upper = pack(pool_owner, halo_blocks, blocks, subs)
    arrived = lax.all_to_all(send, ("mem", "sub"), 0, 0, tiled=True)
    from_lower = lax.ppermute(upper, everyone, [(i, i + 1) for i in range(devices - 1)])
    from_upper = lax.ppermute(lower, everyone, [(i + 1, i) for i in range(devices - 1)])
    messages = block_messages(
        edge_target, edge_source, edge_count, blocks, from_lower, from_upper, edge_tiles
    )

    own_sub = lax.axis_index("sub").astype(jnp.int32)
    sub_index = jnp.concatenate([own_sub[None], (own_sub + pooled_block_source_index) % subs])
    reply = coarse_update(
        sub_index,
        arrived,
        coarse_tiles,
        coarse_first,
        coarse_bias[None],
        coarse_second,
        pooled_level_scale_factor[None],
    )
    returned = lax.all_to_all(reply, "mem", 0, 0, tiled=True)
    partial = fine_update(
        fine_nodes,
        messages.reshape(fine_nodes.shape),
        fine_first,
        fine_bias[None],
        fine_second,
        fine_gain[None],
    )
    return finish(pool_owner, partial, returned)


def solution(mesh):
    dom, sub = mesh.devices.shape
    split = Mesh(mesh.devices.reshape(dom // WIN, WIN, sub), ("win", "mem", "sub"))
    every = ("win", "mem", "sub")
    placed = (
        P(every, None),
        P(every, None, None),
        P(every),
        P(every),
        P(every),
        P(every),
        P(every),
        P(every, None, None),
        P(every),
        P(),
        P(),
        P(),
        P(),
        P(),
        P(),
        P(),
        P(),
    )
    return jax.shard_map(
        per_device, mesh=split, in_specs=placed, out_specs=P(every, None), check_vma=False
    )
```

time: 185 us -> 54.7 us (0.30)
  the two profiles are of different devices: /device:TPU:32 before, /device:TPU:9 now
where the time goes in v1:
time: 54.7 us; the launch traced here: 54.2 us
  starting transfers between devices  23.2 us (42%)
  Pallas kernels  13.4 us (24%)
  local copies, waits for them, and re-layouts  9.59 us (18%)
  waiting for transfers between devices  7.06 us (13%)
  between operations  0.79 us (1%)
    all_to_all x1, starting transfers between devices, per_device(): returned = lax.all_to_all(reply, 'mem', 0, 0, tiled=True)  9.69 us
    unnamed x40, local copies, waits for them, and re-layouts  9.59 us
    all_to_all x1, starting transfers between devices, per_device(): arrived = lax.all_to_all(send, ('mem', 'sub'), 0, 0, tiled=True)  6.8 us
    ppermute x1, waiting for transfers between devices, per_device(): lax.ppermute(upper, everyone, [(i, i + 1) for i in range(devices - 1)])  5.44 us
    pallas_call x1, Pallas kernels, block_messages(): pl.pallas_call(message_kernel, name='messages', out_shape=jax.ShapeDtypeS...  4.14 us
    ppermute x1, starting transfers between devices, per_device(): lax.ppermute(lower, everyone, [(i + 1, i) for i in range(devices - 1)])  3.48 us
    pallas_call x1, Pallas kernels, fine_update(): pl.pallas_call(fine_kernel, name='fine', out_shape=jax.ShapeDtypeStruct(n...  3.38 us
    ppermute x1, starting transfers between devices, per_device(): lax.ppermute(upper, everyone, [(i, i + 1) for i in range(devices - 1)])  3.28 us
  transfers between devices with their start and end apart: 4, of which 2 were waited for; matrix products, arithmetic and copies ran while one was open for 0% of the time, Pallas kernels for 14%

profile of v1, /device:TPU:9, one launch (start us, length us, event | category | flops | bytes accessed | tf_op | source)
XLA Modules:
  0.0 54.2 jit_solution(17424235876802736628)
XLA Ops:
  0.0 1.3 %copy-done = bf16[1024,512]{1,0:T(8,128)(2,1)S(1)} copy-done((bf16[1024,512]{1,0:T(8,128)(2,1)S(1)}, bf16[1024,512]{1,0:T(8,128)(2,1)}, u32[]{:S(2)}) %copy-start) | copy-done | bytes 1048600
  1.3 0.7 %copy-done.7 = s32[8]{0:T(128)S(1)} copy-done((s32[8]{0:T(128)S(1)}, s32[8]{0:T(128)}, u32[]{:S(2)}) %copy-start.7) | copy-done | bytes 56
  1.9 0.7 %copy-done.9 = s32[4]{0:T(128)S(1)} copy-done((s32[4]{0:T(128)S(1)}, s32[4]{0:T(128)}, u32[]{:S(2)}) %copy-start.9) | copy-done | bytes 40
  2.6 1.7 %pack.1 = (bf16[16,9,16,128]{3,2,1,0:T(8,128)(2,1)}, bf16[2,128,512]{2,1,0:T(8,128)(2,1)S(1)}, bf16[2,128,512]{2,1,0:T(8,128)(2,1)S(1)}) custom-call(s32[8]{0:T(128)S(1)} %copy-done.7, s32[4]{0:T(128)S(1)} %copy-done.9, bf16[8,128,512]{2,1,0:T(8,128)(2,1)S(1)} %bitcast.7), custom_call_target="tpu_custom_call" | custom-call | flops 134217728 | bytes 3145728 | tf_op jit(solution)/shard_map/pack/pallas_call | solution.py:66
  4.3 6.8 %all-to-all-start = ((bf16[16,9,16,128]{3,2,1,0:T(8,128)(2,1)}), bf16[16,9,16,128]{3,2,1,0:T(8,128)(2,1)S(1)}, u32[]{:S(2)}, u32[]{:S(2)}) async-start(bf16[16,9,16,128]{3,2,1,0:T(8,128)(2,1)} %get-tuple-element.10), calls=%async_computation | async-start | bytes 1179648 | tf_op jit(solution)/shard_map/all_to_all | solution.py:322
  11.1 3.3 %collective-permute-start = (bf16[2,128,512]{2,1,0:T(8,128)(2,1)S(1)}, bf16[2,128,512]{2,1,0:T(8,128)(2,1)}, u32[]{:S(2)}, u32[]{:S(2)}) collective-permute-start(bf16[2,128,512]{2,1,0:T(8,128)(2,1)S(1)} %get-tuple-element.8), channel_id=1, source_target_pairs={{0,1},{1,2},{2,3},{3,4},{4,5},{5,6},{6,7},{7,8},{8,9},{9,10},{10,1... | collective-permute-start | bytes 786440 | tf_op jit(solution)/shard_map/ppermute | solution.py:323
  14.4 3.5 %collective-permute-start.1 = (bf16[2,128,512]{2,1,0:T(8,128)(2,1)S(1)}, bf16[2,128,512]{2,1,0:T(8,128)(2,1)}, u32[]{:S(2)}, u32[]{:S(2)}) collective-permute-start(bf16[2,128,512]{2,1,0:T(8,128)(2,1)S(1)} %get-tuple-element.9), channel_id=1, source_target_pairs={{1,0},{2,1},{3,2},{4,3},{5,4},{6,5},{7,6},{8,7},{9,8},{10,9},{11,1... | collective-permute-start | bytes 786440 | tf_op jit(solution)/shard_map/ppermute | solution.py:324
  18.5 0.1 pad_add_fusion.sub_ref
  18.6 5.4 %collective-permute-done.lower_ref = bf16[2,128,512]{2,1,0:T(8,128)(2,1)} collective-permute-done((bf16[2,128,512]{2,1,0:T(8,128)(2,1)S(1)}, bf16[2,128,512]{2,1,0:T(8,128)(2,1)}, u32[]{:S(2)}, u32[]{:S(2)}) %collective-permute-start) | collective-permute-done | bytes 262176 | tf_op jit(solution)/shard_map/ppermute | solution.py:323
  24.1 1.6 %collective-permute-done.1.upper_ref = bf16[2,128,512]{2,1,0:T(8,128)(2,1)} collective-permute-done((bf16[2,128,512]{2,1,0:T(8,128)(2,1)S(1)}, bf16[2,128,512]{2,1,0:T(8,128)(2,1)}, u32[]{:S(2)}, u32[]{:S(2)}) %collective-permute-start.1) | collective-permute-done | bytes 262176 | tf_op jit(solution)/shard_map/ppermute | solution.py:324
  25.7 0.0 copy-start.10
  25.7 1.5 %copy-done.10 = bf16[56,128,128]{2,1,0:T(8,128)(2,1)S(1)} copy-done((bf16[56,128,128]{2,1,0:T(8,128)(2,1)S(1)}, bf16[56,128,128]{2,1,0:T(8,128)(2,1)}, u32[]{:S(2)}) %copy-start.10) | copy-done | bytes 1835032
  27.2 4.1 %messages.1 = bf16[8,128,512]{2,1,0:T(8,128)(2,1)S(1)} custom-call(s32[56]{0:T(128)S(1)} %copy-done.15, s32[56]{0:T(128)S(1)} %copy-done.16, s32[1]{0:T(128)S(6)} %copy.18.count_ref, bf16[8,128,512]{2,1,0:T(8,128)(2,1)S(1)} %bitcast.8, bf16[2,128,512]{2,1,0:T(8,128)(2,1)} %collective-permute-done.lower_ref, ...), custom_call_target="tpu_custom_call" | custom-call | flops 4294967296 | bytes 6291456 | tf_op jit(solution)/shard_map/messages/pallas_call | solution.py:225
  31.3 0.0 copy-start.17
  31.4 1.0 %copy-done.17 = bf16[8,128,512]{2,1,0:T(8,128)(2,1)} copy-done((bf16[8,128,512]{2,1,0:T(8,128)(2,1)}, bf16[8,128,512]{2,1,0:T(8,128)(2,1)S(1)}, u32[]{:S(2)}) %copy-start.17) | copy-done | bytes 1048600
  32.3 0.0 copy-start.3
  32.4 1.0 %copy-done.3 = bf16[512,512]{1,0:T(8,128)(2,1)S(1)} copy-done((bf16[512,512]{1,0:T(8,128)(2,1)S(1)}, bf16[512,512]{1,0:T(8,128)(2,1)}, u32[]{:S(2)}) %copy-start.3) | copy-done | bytes 524312
  33.4 2.3 %coarse.1 = bf16[4,2,16,512]{3,2,1,0:T(8,128)(2,1)} custom-call(s32[3]{0:T(128)S(1)} %pad_add_fusion.sub_ref, bf16[16,9,16,128]{3,2,1,0:T(8,128)(2,1)S(1)} %all-to-all-done.arrived_ref, bf16[2,128,128]{2,1,0:T(8,128)(2,1)S(1)} %copy-done.4, bf16[1024,512]{1,0:T(8,128)(2,1)S(1)} %copy-done.2, f32[1,512]{1,0:T(1,128)S(1)} %bitcast.9, ...), custom_call_target="tpu_custom_call" | custom-call | flops 536870912 | bytes 3145728 | tf_op jit(solution)/shard_map/coarse/pallas_call | solution.py:148
  35.6 9.7 %all-to-all-start.1 = ((bf16[4,2,16,512]{3,2,1,0:T(8,128)(2,1)}), bf16[4,2,16,512]{3,2,1,0:T(8,128)(2,1)S(1)}, u32[]{:S(2)}, u32[]{:S(2)}) async-start(bf16[4,2,16,512]{3,2,1,0:T(8,128)(2,1)} %coarse.1), calls=%async_computation.1 | async-start | bytes 262144 | tf_op jit(solution)/shard_map/all_to_all | solution.py:340
  45.3 1.2 %copy-done.11 = bf16[1024,512]{1,0:T(8,128)(2,1)S(1)} copy-done((bf16[1024,512]{1,0:T(8,128)(2,1)S(1)}, bf16[1024,512]{1,0:T(8,128)(2,1)}, u32[]{:S(2)}) %copy-start.11) | copy-done | bytes 1048600
  46.6 1.0 %copy-done.12 = bf16[512,512]{1,0:T(8,128)(2,1)S(1)} copy-done((bf16[512,512]{1,0:T(8,128)(2,1)S(1)}, bf16[512,512]{1,0:T(8,128)(2,1)}, u32[]{:S(2)}) %copy-start.12) | copy-done | bytes 524312
  47.6 1.2 %copy-done.18 = bf16[8,128,512]{2,1,0:T(8,128)(2,1)S(1)} copy-done((bf16[8,128,512]{2,1,0:T(8,128)(2,1)S(1)}, bf16[8,128,512]{2,1,0:T(8,128)(2,1)}, u32[]{:S(2)}) %copy-start.18) | copy-done | bytes 1048600
  48.8 3.4 %fine.1.partial_ref = f32[1024,512]{1,0:T(8,128)S(1)} custom-call(bf16[1024,512]{1,0:T(8,128)(2,1)S(1)} %copy-done.1, bf16[1024,512]{1,0:T(8,128)(2,1)S(1)} %bitcast.13, bf16[1024,512]{1,0:T(8,128)(2,1)S(1)} %copy-done.11, f32[1,512]{1,0:T(1,128)S(1)} %bitcast.11, bf16[512,512]{1,0:T(8,128)(2,1)S(1)} %copy-done.12, f32[1,512]{1,0:T(1,128)S(1)} %bitcast.12), custom_call_target="tpu_custom_call" | custom-call | flops 2147483648 | bytes 6291456 | tf_op jit(solution)/shard_map/fine/pallas_call | solution.py:257
  52.2 1.9 %finish.1 = bf16[1024,512]{1,0:T(8,128)(2,1)} custom-call(s32[8]{0:T(128)S(1)} %copy-done.8, f32[1024,512]{1,0:T(8,128)S(1)} %fine.1.partial_ref, bf16[4,2,16,512]{3,2,1,0:T(8,128)(2,1)S(1)} %all-to-all-done.1.reply_ref), custom_call_target="tpu_custom_call" | custom-call | flops 33554432 | bytes 4194304 | tf_op jit(solution)/shard_map/finish/pallas_call | solution.py:282
  (31 shorter events, 0.1 us)
Async XLA Ops:
  0.0 18.5 %copy-start.19 = (s32[2]{0:T(128)S(1)}, s32[2]{0:T(128)}, u32[]{:S(2)}) copy-start(s32[2]{0:T(128)} %param.25) | copy-start | bytes 28
  0.0 25.7 %copy-start.16 = (s32[56]{0:T(128)S(1)}, s32[56]{0:T(128)}, u32[]{:S(2)}) copy-start(s32[56]{0:T(128)} %source_ref.1) | copy-start | bytes 676
  0.0 25.7 %copy-start.15 = (s32[56]{0:T(128)S(1)}, s32[56]{0:T(128)}, u32[]{:S(2)}) copy-start(s32[56]{0:T(128)} %target_ref.1) | copy-start | bytes 676
  0.0 1.3 %copy-start = (bf16[1024,512]{1,0:T(8,128)(2,1)S(1)}, bf16[1024,512]{1,0:T(8,128)(2,1)}, u32[]{:S(2)}) copy-start(bf16[1024,512]{1,0:T(8,128)(2,1)} %nodes_ref.1) | copy-start | bytes 3145732
  1.3 0.7 %copy-start.7 = (s32[8]{0:T(128)S(1)}, s32[8]{0:T(128)}, u32[]{:S(2)}) copy-start(s32[8]{0:T(128)} %owner_ref.3) | copy-start | bytes 100
  1.9 0.7 %copy-start.9 = (s32[4]{0:T(128)S(1)}, s32[4]{0:T(128)}, u32[]{:S(2)}) copy-start(s32[4]{0:T(128)} %halo_ref.1) | copy-start | bytes 52
  2.6 23.1 %copy-start.1 = (bf16[1024,512]{1,0:T(8,128)(2,1)S(1)}, bf16[1024,512]{1,0:T(8,128)(2,1)}, u32[]{:S(2)}) copy-start(bf16[1024,512]{1,0:T(8,128)(2,1)} %nodes_ref.1) | copy-start | bytes 3145732
  4.3 28.0 %all-to-all-start = ((bf16[16,9,16,128]{3,2,1,0:T(8,128)(2,1)}), bf16[16,9,16,128]{3,2,1,0:T(8,128)(2,1)S(1)}, u32[]{:S(2)}, u32[]{:S(2)}) async-start(bf16[16,9,16,128]{3,2,1,0:T(8,128)(2,1)} %get-tuple-element.10), calls=%async_computation | async-start | bytes 1179648 | tf_op jit(solution)/shard_map/all_to_all | solution.py:322
  11.1 13.0 %collective-permute-start = (bf16[2,128,512]{2,1,0:T(8,128)(2,1)S(1)}, bf16[2,128,512]{2,1,0:T(8,128)(2,1)}, u32[]{:S(2)}, u32[]{:S(2)}) collective-permute-start(bf16[2,128,512]{2,1,0:T(8,128)(2,1)S(1)} %get-tuple-element.8), channel_id=1, source_target_pairs={{0,1},{1,2},{2,3},{3,4},{4,5},{5,6},{6,7},{7,8},{8,9},{9,10},{10,1... | collective-permute-start | bytes 786440 | tf_op jit(solution)/shard_map/ppermute | solution.py:323
  14.4 11.3 %collective-permute-start.1 = (bf16[2,128,512]{2,1,0:T(8,128)(2,1)S(1)}, bf16[2,128,512]{2,1,0:T(8,128)(2,1)}, u32[]{:S(2)}, u32[]{:S(2)}) collective-permute-start(bf16[2,128,512]{2,1,0:T(8,128)(2,1)S(1)} %get-tuple-element.9), channel_id=1, source_target_pairs={{1,0},{2,1},{3,2},{4,3},{5,4},{6,5},{7,6},{8,7},{9,8},{10,9},{11,1... | collective-permute-start | bytes 786440 | tf_op jit(solution)/shard_map/ppermute | solution.py:324
  18.6 13.7 %copy-start.2 = (bf16[1024,512]{1,0:T(8,128)(2,1)S(1)}, bf16[1024,512]{1,0:T(8,128)(2,1)}, u32[]{:S(2)}) copy-start(bf16[1024,512]{1,0:T(8,128)(2,1)} %first_ref.3) | copy-start | bytes 3145732
  18.6 13.7 %copy-start.4 = (bf16[2,128,128]{2,1,0:T(8,128)(2,1)S(1)}, bf16[2,128,128]{2,1,0:T(8,128)(2,1)}, u32[]{:S(2)}) copy-start(bf16[2,128,128]{2,1,0:T(8,128)(2,1)} %tiles_ref.1) | copy-start | bytes 196612
  18.6 13.7 %copy-start.5 = (f32[512]{0:T(512)S(1)}, f32[512]{0:T(512)}, u32[]{:S(2)}) copy-start(f32[512]{0:T(512)} %param.31) | copy-start | bytes 6148
  18.6 13.7 %copy-start.6 = (f32[512]{0:T(512)S(1)}, f32[512]{0:T(512)}, u32[]{:S(2)}) copy-start(f32[512]{0:T(512)} %param.33) | copy-start | bytes 6148
  25.7 1.5 %copy-start.10 = (bf16[56,128,128]{2,1,0:T(8,128)(2,1)S(1)}, bf16[56,128,128]{2,1,0:T(8,128)(2,1)}, u32[]{:S(2)}) copy-start(bf16[56,128,128]{2,1,0:T(8,128)(2,1)} %edges_ref.1) | copy-start | bytes 5505028
  27.2 18.1 %copy-start.14 = (f32[512]{0:T(512)S(1)}, f32[512]{0:T(512)}, u32[]{:S(2)}) copy-start(f32[512]{0:T(512)} %param.29) | copy-start | bytes 6148
  31.3 1.0 %copy-start.17 = (bf16[8,128,512]{2,1,0:T(8,128)(2,1)}, bf16[8,128,512]{2,1,0:T(8,128)(2,1)S(1)}, u32[]{:S(2)}) copy-start(bf16[8,128,512]{2,1,0:T(8,128)(2,1)S(1)} %messages.1) | copy-start | bytes 3145732
  32.3 13.0 %copy-start.13 = (f32[512]{0:T(512)S(1)}, f32[512]{0:T(512)}, u32[]{:S(2)}) copy-start(f32[512]{0:T(512)} %param.27) | copy-start | bytes 6148
  32.3 1.0 %copy-start.3 = (bf16[512,512]{1,0:T(8,128)(2,1)S(1)}, bf16[512,512]{1,0:T(8,128)(2,1)}, u32[]{:S(2)}) copy-start(bf16[512,512]{1,0:T(8,128)(2,1)} %second_ref.3) | copy-start | bytes 1572868
  35.6 16.6 %all-to-all-start.1 = ((bf16[4,2,16,512]{3,2,1,0:T(8,128)(2,1)}), bf16[4,2,16,512]{3,2,1,0:T(8,128)(2,1)S(1)}, u32[]{:S(2)}, u32[]{:S(2)}) async-start(bf16[4,2,16,512]{3,2,1,0:T(8,128)(2,1)} %coarse.1), calls=%async_computation.1 | async-start | bytes 262144 | tf_op jit(solution)/shard_map/all_to_all | solution.py:340
  45.3 1.2 %copy-start.11 = (bf16[1024,512]{1,0:T(8,128)(2,1)S(1)}, bf16[1024,512]{1,0:T(8,128)(2,1)}, u32[]{:S(2)}) copy-start(bf16[1024,512]{1,0:T(8,128)(2,1)} %first_ref.2) | copy-start | bytes 3145732
  46.6 1.0 %copy-start.12 = (bf16[512,512]{1,0:T(8,128)(2,1)S(1)}, bf16[512,512]{1,0:T(8,128)(2,1)}, u32[]{:S(2)}) copy-start(bf16[512,512]{1,0:T(8,128)(2,1)} %second_ref.2) | copy-start | bytes 1572868
  47.6 1.2 %copy-start.18 = (bf16[8,128,512]{2,1,0:T(8,128)(2,1)S(1)}, bf16[8,128,512]{2,1,0:T(8,128)(2,1)}, u32[]{:S(2)}) copy-start(bf16[8,128,512]{2,1,0:T(8,128)(2,1)} %copy-done.17) | copy-start | bytes 3145732
  48.8 3.4 %copy-start.8 = (s32[8]{0:T(128)S(1)}, s32[8]{0:T(128)}, u32[]{:S(2)}) copy-start(s32[8]{0:T(128)} %owner_ref.3) | copy-start | bytes 100

commit v2 on v1

v2 whole, which is shorter than its diff:
```python
import jax
import jax.numpy as jnp
from jax import lax
from jax.experimental import pallas as pl
from jax.experimental.pallas import tpu as pltpu
from jax.sharding import Mesh
from jax.sharding import PartitionSpec as P

POOL = 8
WIN = 4
ROW = 64
DEPTH = 2
SIDE = 2
F32 = jnp.float32
BF16 = jnp.bfloat16

VMEM_SPEC = pl.BlockSpec(memory_space=pltpu.VMEM)
SMEM_SPEC = pl.BlockSpec(memory_space=pltpu.SMEM)
HBM_SPEC = pl.BlockSpec(memory_space=pltpu.HBM)
ANY_SPEC = pl.BlockSpec(memory_space=pl.ANY)


def room_for(*arrays):
    taken = sum(array.size * array.dtype.itemsize for array in arrays)
    return pltpu.CompilerParams(vmem_limit_bytes=(64 << 20) - taken)


PARAMS = room_for()


def started(pairs, sems):
    copies = [pltpu.make_async_copy(src, dst, sems.at[i]) for i, (src, dst) in enumerate(pairs)]
    for copy in copies:
        copy.start()
    return copies


def owner_slots(owner_ref, count_ref, block_count):
    for d in range(WIN):
        count_ref[d] = 0
    slots = []
    for k in range(block_count):
        d = owner_ref[k] & (WIN - 1)
        r = count_ref[d]
        count_ref[d] = r + 1
        slots.append((d, r))
    return slots


def pack_kernel(
    owner_hbm, halo_hbm, nodes_hbm, send_hbm, lower_hbm, upper_hbm,
    owner_ref, halo_ref, nodes_ref, send_ref, count_ref, index_ref, int_sems, node_sems, halo_sems, send_sems,
):
    blocks, rows, width = nodes_ref.shape
    tile = rows // POOL
    lanes = send_ref.shape[-1]
    groups = width // lanes
    subs = send_hbm.shape[0] // WIN
    halo = halo_ref.shape[0] // 2
    ints = started([(owner_hbm, owner_ref), (halo_hbm, halo_ref)], int_sems)
    loads = started([(nodes_hbm.at[k], nodes_ref.at[k]) for k in range(blocks)], node_sems)
    for copy in ints:
        copy.wait()
    row = lax.broadcasted_iota(jnp.int32, (tile, rows), 0)
    col = lax.broadcasted_iota(jnp.int32, (tile, rows), 1)
    average = jnp.where(col // POOL == row, 1.0 / POOL, 0.0).astype(BF16)
    slots = owner_slots(owner_ref, count_ref, blocks)
    for k, (d, r) in enumerate(slots):
        index_ref[d * 2 + r] = k
    lane = lax.broadcasted_iota(jnp.int32, (tile, lanes), 1)
    for d in range(WIN):
        tag = jnp.where((lane // tile) % 2 == 0, index_ref[2 * d], index_ref[2 * d + 1])
        send_ref[d, groups * 2] = tag.astype(F32).astype(BF16)
    for k, (d, r) in enumerate(slots):
        loads[k].wait()
        pooled = jnp.dot(average, nodes_ref[k], preferred_element_type=F32).astype(BF16)
        for c in range(groups):
            send_ref[d, c * 2 + r] = pooled[:, c * lanes : (c + 1) * lanes]
    halos = started(
        [(nodes_ref.at[halo_ref[h]], lower_hbm.at[h]) for h in range(halo)]
        + [(nodes_ref.at[halo_ref[halo + h]], upper_hbm.at[h]) for h in range(halo)],
        halo_sems,
    )
    sends = started(
        [(send_ref.at[d], send_hbm.at[d * subs + s]) for d in range(WIN) for s in range(subs)], send_sems
    )
    for copy in halos + sends:
        copy.wait()


def pack(pool_owner, halo_blocks, blocks, subs):
    count, rows, width = blocks.shape
    tile = rows // POOL
    halos = halo_blocks.shape[0]
    lanes = 128
    pieces = 2 * (width // lanes) + 1
    return pl.pallas_call(
        pack_kernel,
        name="pack",
        out_shape=(
            jax.ShapeDtypeStruct((WIN * subs, pieces, tile, lanes), BF16),
            jax.ShapeDtypeStruct((halos // 2, rows, width), BF16),
            jax.ShapeDtypeStruct((halos // 2, rows, width), BF16),
        ),
        in_specs=[HBM_SPEC] * 3,
        out_specs=(ANY_SPEC,) * 3,
        scratch_shapes=[
            pltpu.SMEM((count,), jnp.int32),
            pltpu.SMEM((halos,), jnp.int32),
            pltpu.VMEM(blocks.shape, BF16),
            pltpu.VMEM((WIN, pieces, tile, lanes), BF16),
            pltpu.SMEM((WIN,), jnp.int32),
            pltpu.SMEM((2 * WIN,), jnp.int32),
            pltpu.SemaphoreType.DMA((2,)),
            pltpu.SemaphoreType.DMA((count,)),
            pltpu.SemaphoreType.DMA((halos,)),
            pltpu.SemaphoreType.DMA((WIN * subs,)),
        ],
        compiler_params=PARAMS,
        cost_estimate=pl.CostEstimate(flops=1 << 27, bytes_accessed=3 << 20, transcendentals=0),
    )(pool_owner, halo_blocks, blocks)


def normalised(values, gain):
    row_mean = jnp.mean(values, axis=-1, keepdims=True)
    centred = values - row_mean
    variance = jnp.mean(centred * centred, axis=-1, keepdims=True)
    return centred * lax.rsqrt(variance + 1e-05) * gain


def network(nodes, messages, first_ref, bias_ref, second_ref, gain_ref):
    width = nodes.shape[1]
    hidden = jnp.dot(nodes, first_ref[:width], preferred_element_type=F32)
    hidden += jnp.dot(messages, first_ref[width:], preferred_element_type=F32)
    hidden = jnp.maximum(hidden + bias_ref[...], 0.0).astype(BF16)
    projected = jnp.dot(hidden, second_ref[...], preferred_element_type=F32)
    return normalised(projected, gain_ref[...])


def coarse_kernel(
    sub_ref, offset_hbm, arrived_hbm, tiles_hbm, first_hbm, bias_hbm, second_hbm, gain_hbm, after_hbm, reply_hbm,
    offset_ref, arrived_ref, tiles_ref, first_ref, bias_ref, second_ref, gain_ref, reply_ref, sems,
):
    senders, pieces, tile, lanes = arrived_ref.shape
    groups = pieces // 2
    subs = senders // WIN
    entries, rows, _ = tiles_ref.shape
    loads = started(
        [
            (offset_hbm, offset_ref),
            (arrived_hbm, arrived_ref),
            (tiles_hbm, tiles_ref),
            (first_hbm, first_ref),
            (bias_hbm, bias_ref.at[0]),
            (second_hbm, second_ref),
            (gain_hbm, gain_ref.at[0]),
        ],
        sems,
    )
    row = lax.broadcasted_iota(jnp.int32, (rows, rows), 0)
    col = lax.broadcasted_iota(jnp.int32, (rows, rows), 1)
    same_row = row % tile == col % tile

    def arrived_rows(s):
        return jnp.concatenate(
            [
                jnp.concatenate([arrived_ref[m * subs + s, c * 2 + r] for c in range(groups)], axis=1)
                for m in range(WIN)
                for r in range(2)
            ],
            axis=0,
        )

    def placing(s):
        tags = jnp.zeros((8, lanes), F32)
        lane = lax.broadcasted_iota(jnp.int32, (8, lanes), 1)
        for m in range(WIN):
            tag = arrived_ref[m * subs + s, groups * 2].astype(F32)[:8]
            tags = jnp.where(lane // (2 * tile) == m, tag, tags)
        return jnp.where(same_row & (row // tile == tags[:1].astype(jnp.int32)), 1.0, 0.0)

    own = sub_ref[0]
    for copy in loads[:3]:
        copy.wait()
    own_rows = arrived_rows(own)
    own_back = placing(own).T.astype(BF16)
    weights, sources = [], []
    for e in range(entries):
        s = lax.rem(own + offset_ref[e], subs)
        sources.append(arrived_rows(s))
        by_col = jnp.dot(tiles_ref[e], placing(s).astype(BF16), preferred_element_type=F32)
        weights.append(by_col.astype(BF16))
    by_col = jnp.concatenate(weights, axis=1)
    by_both = jnp.dot(own_back, by_col, preferred_element_type=F32).astype(BF16)
    messages = jnp.dot(by_both, jnp.concatenate(sources, axis=0), preferred_element_type=F32)
    for copy in loads[3:]:
        copy.wait()
    delta = network(own_rows, messages.astype(BF16), first_ref, bias_ref, second_ref, gain_ref)
    delta = delta.astype(BF16)
    for m in range(WIN):
        for r in range(2):
            at = (m * 2 + r) * tile
            reply_ref[m, r] = delta[at : at + tile]
    out = pltpu.make_async_copy(reply_ref, reply_hbm, sems.at[0])
    out.start()
    out.wait()


def coarse_update(own_sub, offsets, arrived, tiles, first, bias, second, gain, after):
    width = second.shape[0]
    tile = arrived.shape[2]
    reply = jax.ShapeDtypeStruct((WIN, 2, tile, width), BF16)
    return pl.pallas_call(
        coarse_kernel,
        name="coarse",
        out_shape=reply,
        in_specs=[SMEM_SPEC, HBM_SPEC, ANY_SPEC] + [HBM_SPEC] * 5 + [ANY_SPEC],
        out_specs=ANY_SPEC,
        scratch_shapes=[
            pltpu.SMEM(offsets.shape, jnp.int32),
            pltpu.VMEM(arrived.shape, BF16),
            pltpu.VMEM(tiles.shape, BF16),
            pltpu.VMEM(first.shape, BF16),
            pltpu.VMEM((1, width), F32),
            pltpu.VMEM(second.shape, BF16),
            pltpu.VMEM((1, width), F32),
            pltpu.VMEM(reply.shape, BF16),
            pltpu.SemaphoreType.DMA((7,)),
        ],
        compiler_params=room_for(arrived),
        cost_estimate=pl.CostEstimate(flops=1 << 29, bytes_accessed=3 << 20, transcendentals=0),
    )(own_sub, offsets, arrived, tiles, first, bias, second, gain, after)


def add_messages(
    target_ref, source_ref, live, table, tiles, total, order, place, loads
):
    blocks = total.shape[0]
    entries = target_ref.shape[0]
    slots = order.shape[0]
    for b in range(blocks + 1):
        place[b] = 0
    for i in range(slots):
        order[i] = entries
    bins = []
    for e in range(entries):
        b = jnp.where(e < live, target_ref[e], blocks)
        place[b] = place[b] + 1
        bins.append(b)
    at = 0
    for b in range(blocks):
        steps = (place[b] + (DEPTH - 1)) // DEPTH
        place[b] = at * DEPTH
        at = at + steps
    place[blocks] = slots - entries
    used = at
    for e in range(entries):
        at = place[bins[e]]
        place[bins[e]] = at + 1
        order[at] = e + (source_ref[e] << 8) + (bins[e] << 16)
    for copy in loads:
        copy.wait()

    @pl.loop(0, (used + (SIDE - 1)) // SIDE)
    def _(i):
        products = []
        for u in range(SIDE):
            codes = [order[(i * SIDE + u) * DEPTH + g] for g in range(DEPTH)]
            left = jnp.concatenate([tiles[code & 255] for code in codes], axis=1)
            right = jnp.concatenate([table[(code >> 8) & 255] for code in codes], axis=0)
            product = jnp.dot(left, right, preferred_element_type=F32)
            products.append((codes[0] >> 16, product))
        for b, product in products:
            total[b] += product


def order_slots(entries, blocks):
    groups = entries // DEPTH + blocks
    return (groups + SIDE - 1) // SIDE * SIDE * DEPTH + entries


def fine_body(
    target_hbm, source_hbm, count_ref, lower_hbm, upper_hbm, edges_hbm, nodes_hbm,
    first_hbm, bias_hbm, second_hbm, gain_hbm, out_hbm,
    target_ref, source_ref, table, tiles, total, order, place,
    first_ref, bias_ref, second_ref, gain_ref, out_ref, sems, out_sems,
):
    entries = edges_hbm.shape[0]
    halo = lower_hbm.shape[0]
    blocks, rows, width = total.shape
    loads = started(
        [
            (target_hbm, target_ref),
            (source_hbm, source_ref),
            (edges_hbm, tiles.at[pl.ds(0, entries)]),
            (nodes_hbm, table.at[pl.ds(0, blocks)]),
            (lower_hbm, table.at[pl.ds(blocks, halo)]),
            (upper_hbm, table.at[pl.ds(blocks + halo, halo)]),
            (first_hbm, first_ref),
            (second_hbm, second_ref),
            (bias_hbm, bias_ref.at[0]),
            (gain_hbm, gain_ref.at[0]),
        ],
        sems,
    )
    tiles[entries] = jnp.zeros(tiles.shape[1:], BF16)
    total[...] = jnp.zeros_like(total)
    for copy in loads[:2]:
        copy.wait()
    add_messages(target_ref, source_ref, count_ref[0], table, tiles, total, order, place, loads[2:6])
    for copy in loads[6:]:
        copy.wait()
    outs = []
    for i in range(blocks // 2):
        at = pl.ds(2 * i, 2)
        nodes = table[2 * i : 2 * i + 2].reshape(2 * rows, width)
        messages = total[2 * i : 2 * i + 2].reshape(2 * rows, width).astype(BF16)
        delta = network(nodes, messages, first_ref, bias_ref, second_ref, gain_ref)
        out_ref[2 * i : 2 * i + 2] = (nodes.astype(F32) + delta).reshape(2, rows, width)
        outs += started([(out_ref.at[at], out_hbm.at[at])], out_sems.at[pl.ds(i, 1)])
    for out in outs:
        out.wait()


def fine_kernel(late_ref, *refs):
    @pl.when(late_ref[0] == 0)
    def _():
        fine_body(*refs)


def late_kernel(late_ref, done_hbm, after_hbm, *refs):
    @pl.when(late_ref[0] == 1)
    def _():
        fine_body(*refs)


def fine_update(late, entries, lower, upper, edges, nodes, first, bias, second, gain, done=None, after=None):
    entry_count, rows, _ = edges.shape
    block_count, _, width = nodes.shape
    halo = lower.shape[0]
    target, source, count = entries
    held = [] if done is None else [done, after]
    return pl.pallas_call(
        fine_kernel if done is None else late_kernel,
        name="fine" if done is None else "late",
        out_shape=jax.ShapeDtypeStruct(nodes.shape, F32),
        in_specs=[SMEM_SPEC]
        + [ANY_SPEC] * len(held)
        + [HBM_SPEC, HBM_SPEC, SMEM_SPEC, ANY_SPEC, ANY_SPEC]
        + [HBM_SPEC] * 6,
        out_specs=ANY_SPEC,
        input_output_aliases={1: 0} if held else {},
        scratch_shapes=[
            pltpu.SMEM((entry_count,), jnp.int32),
            pltpu.SMEM((entry_count,), jnp.int32),
            pltpu.VMEM((block_count + 2 * halo, rows, width), BF16),
            pltpu.VMEM((entry_count + 1, rows, rows), BF16),
            pltpu.VMEM(nodes.shape, F32),
            pltpu.SMEM((order_slots(entry_count, block_count),), jnp.int32),
            pltpu.SMEM((block_count + 1,), jnp.int32),
            pltpu.VMEM(first.shape, BF16),
            pltpu.VMEM((1, width), F32),
            pltpu.VMEM(second.shape, BF16),
            pltpu.VMEM((1, width), F32),
            pltpu.VMEM(nodes.shape, F32),
            pltpu.SemaphoreType.DMA((10,)),
            pltpu.SemaphoreType.DMA((block_count // 2,)),
        ],
        compiler_params=PARAMS,
        cost_estimate=pl.CostEstimate(
            flops=1 << (20 if held else 37), bytes_accessed=1 << 20, transcendentals=0
        ),
    )(late, *held, target, source, count, lower, upper, edges, nodes, first, bias, second, gain)


def finish_kernel(
    owner_hbm, partial_hbm, reply_hbm, out_hbm,
    owner_ref, partial_ref, reply_ref, out_ref, count_ref, sems, in_sems, out_sems,
):
    blocks, rows, _ = partial_ref.shape
    tile = rows // POOL
    loads = started([(owner_hbm, owner_ref), (reply_hbm, reply_ref)], sems)
    pairs = [pl.ds(2 * i, 2) for i in range(blocks // 2)]
    parts = started([(partial_hbm.at[at], partial_ref.at[at]) for at in pairs], in_sems)
    row = lax.broadcasted_iota(jnp.int32, (rows, tile), 0)
    col = lax.broadcasted_iota(jnp.int32, (rows, tile), 1)
    spread = jnp.where(row // POOL == col, 1.0, 0.0).astype(BF16)
    for copy in loads:
        copy.wait()
    slots = owner_slots(owner_ref, count_ref, blocks)
    outs = []
    for i, at in enumerate(pairs):
        parts[i].wait()
        for k in (2 * i, 2 * i + 1):
            d, r = slots[k]
            back = jnp.dot(spread, reply_ref[d, r], preferred_element_type=F32)
            out_ref[k] = (partial_ref[k] + back).astype(BF16)
        outs += started([(out_ref.at[at], out_hbm.at[at])], out_sems.at[pl.ds(i, 1)])
    for out in outs:
        out.wait()


def finish(pool_owner, partial, reply):
    blocks = pool_owner.shape[0]
    return pl.pallas_call(
        finish_kernel,
        name="finish",
        out_shape=jax.ShapeDtypeStruct(partial.shape, BF16),
        in_specs=[HBM_SPEC, ANY_SPEC, ANY_SPEC],
        out_specs=ANY_SPEC,
        scratch_shapes=[
            pltpu.SMEM((blocks,), jnp.int32),
            pltpu.VMEM(partial.shape, F32),
            pltpu.VMEM(reply.shape, BF16),
            pltpu.VMEM(partial.shape, BF16),
            pltpu.SMEM((WIN,), jnp.int32),
            pltpu.SemaphoreType.DMA((2,)),
            pltpu.SemaphoreType.DMA((blocks // 2,)),
            pltpu.SemaphoreType.DMA((blocks // 2,)),
        ],
        compiler_params=room_for(reply),
        cost_estimate=pl.CostEstimate(flops=1 << 25, bytes_accessed=4 << 20, transcendentals=0),
    )(pool_owner, partial, reply)


def per_device(
    fine_nodes,
    edge_tiles,
    edge_target,
    edge_source,
    edge_count,
    halo_blocks,
    pool_owner,
    coarse_tiles,
    pooled_block_source_index,
    fine_first,
    fine_bias,
    fine_second,
    fine_gain,
    coarse_first,
    coarse_bias,
    coarse_second,
    pooled_level_scale_factor,
):
    block_count = pool_owner.shape[0]
    rows = edge_tiles.shape[1]
    width = fine_nodes.shape[1]
    subs = lax.axis_size("sub")
    everyone = ("win", "mem", "sub")
    devices = lax.axis_size(everyone)
    blocks = fine_nodes.reshape(block_count, rows, width)

    own_sub = lax.axis_index("sub").astype(jnp.int32)[None]
    index = lax.axis_index(everyone)
    late = ((index % ROW == ROW - 1) & (index < devices - 1)).astype(jnp.int32)[None]
    send, lower, upper = pack(pool_owner, halo_blocks, blocks, subs)
    from_lower = lax.ppermute(upper, everyone, [(i, i + 1) for i in range(devices - 1)])
    from_upper = lax.ppermute(
        lower, everyone, [(i + 1, i) for i in range(devices - 1) if (i + 1) % ROW]
    )
    arrived = lax.all_to_all(send, ("mem", "sub"), 0, 0, tiled=True)
    entries = (edge_target, edge_source, edge_count)
    network_in = (edge_tiles, blocks, fine_first, fine_bias, fine_second, fine_gain)
    done = fine_update(late, entries, from_lower, from_upper, *network_in)
    lower, done = lax.optimization_barrier((lower, done))
    late_upper = lax.ppermute(lower, everyone, [(i, i - 1) for i in range(ROW, devices, ROW)])
    reply = coarse_update(
        own_sub,
        pooled_block_source_index,
        arrived,
        coarse_tiles,
        coarse_first,
        coarse_bias,
        coarse_second,
        pooled_level_scale_factor,
        done,
    )
    returned = lax.all_to_all(reply, "mem", 0, 0, tiled=True)
    partial = fine_update(late, entries, from_lower, late_upper, *network_in, done=done, after=reply)
    return finish(pool_owner, partial, returned).reshape(fine_nodes.shape)


def solution(mesh):
    dom, sub = mesh.devices.shape
    split = Mesh(mesh.devices.reshape(dom // WIN, WIN, sub), ("win", "mem", "sub"))
    every = ("win", "mem", "sub")
    placed = (
        P(every, None),
        P(every, None, None),
        P(every),
        P(every),
        P(every),
        P(every),
        P(every),
        P(every, None, None),
        P(every),
        P(),
        P(),
        P(),
        P(),
        P(),
        P(),
        P(),
        P(),
    )
    return jax.shard_map(
        per_device, mesh=split, in_specs=placed, out_specs=P(every, None), check_vma=False
    )
```

time: 54.7 us -> 46.7 us (0.85)
  the two profiles are of different devices: /device:TPU:9 before, /device:TPU:191 now
where the time goes in v2:
time: 46.7 us; the launch traced here: 46.3 us
  starting transfers between devices  25 us (54%)
  Pallas kernels  15.8 us (34%)
  waiting for transfers between devices  4.76 us (10%)
  between operations  0.71 us (2%)
    all_to_all x1, starting transfers between devices, per_device(): returned = lax.all_to_all(reply, 'mem', 0, 0, tiled=True)  9.9 us
    all_to_all x1, starting transfers between devices, per_device(): arrived = lax.all_to_all(send, ('mem', 'sub'), 0, 0, tiled=True)  7.31 us
    pallas_call x2, Pallas kernels, fine_update(): pl.pallas_call(fine_kernel if done is None else late_kernel, name='fine'...  6.83 us
    ppermute x1, starting transfers between devices, per_device(): lax.ppermute(upper, everyone, [(i, i + 1) for i in range(devices - 1)])  4.48 us
    all_to_all x1, waiting for transfers between devices, per_device(): returned = lax.all_to_all(reply, 'mem', 0, 0, tiled=True)  4.46 us
    pallas_call x1, Pallas kernels, pack(): pl.pallas_call(pack_kernel, name='pack', out_shape=(jax.ShapeDtypeStruct(...  3.09 us
    pallas_call x1, Pallas kernels, finish(): pl.pallas_call(finish_kernel, name='finish', out_shape=jax.ShapeDtypeStru...  2.97 us
    pallas_call x1, Pallas kernels, coarse_update(): pl.pallas_call(coarse_kernel, name='coarse', out_shape=reply, in_specs=[S...  2.96 us
  transfers between devices with their start and end apart: 5, of which 3 were waited for; matrix products, arithmetic and copies ran while one was open for 0% of the time, Pallas kernels for 21%

profile of v2, /device:TPU:191, one launch (start us, length us, event | category | flops | bytes accessed | tf_op | source)
XLA Modules:
  0.0 46.3 jit_solution(4861415147612895071)
XLA Ops:
  0.0 3.1 %pack.1 = (bf16[16,9,16,128]{3,2,1,0:T(8,128)(2,1)}, bf16[2,128,512]{2,1,0:T(8,128)(2,1)}, bf16[2,128,512]{2,1,0:T(8,128)(2,1)}) custom-call(s32[8]{0:T(128)} %owner_hbm.3, s32[4]{0:T(128)} %halo_hbm.1, bf16[8,128,512]{2,1,0:T(8,128)(2,1)} %bitcast.4), custom_call_target="tpu_custom_call" | custom-call | flops 134217728 | bytes 3145728 | tf_op jit(solution)/shard_map/pack/pallas_call | solution.py:97
  3.1 4.5 %collective-permute-start = (bf16[2,128,512]{2,1,0:T(8,128)(2,1)}, bf16[2,128,512]{2,1,0:T(8,128)(2,1)}, u32[]{:S(2)}, u32[]{:S(2)}) collective-permute-start(bf16[2,128,512]{2,1,0:T(8,128)(2,1)} %get-tuple-element.11), channel_id=1, source_target_pairs={{0,1},{1,2},{2,3},{3,4},{4,5},{5,6},{6,7},{7,8},{8,9},{9,10},{10,1... | collective-permute-start | bytes 786440 | tf_op jit(solution)/shard_map/ppermute | solution.py:457
  7.6 1.9 %collective-permute-start.1 = (bf16[2,128,512]{2,1,0:T(8,128)(2,1)}, bf16[2,128,512]{2,1,0:T(8,128)(2,1)}, u32[]{:S(2)}, u32[]{:S(2)}) collective-permute-start(bf16[2,128,512]{2,1,0:T(8,128)(2,1)} %get-tuple-element.14), channel_id=1, source_target_pairs={{1,0},{2,1},{3,2},{4,3},{5,4},{6,5},{7,6},{8,7},{9,8},{10,9},{11,1... | collective-permute-start | bytes 786440 | tf_op jit(solution)/shard_map/ppermute | solution.py:458
  9.5 7.3 %all-to-all-start = ((bf16[16,9,16,128]{3,2,1,0:T(8,128)(2,1)}), bf16[16,9,16,128]{3,2,1,0:T(8,128)(2,1)}, u32[]{:S(2)}, u32[]{:S(2)}) async-start(bf16[16,9,16,128]{3,2,1,0:T(8,128)(2,1)} %get-tuple-element.13), calls=%async_computation | async-start | bytes 1179648 | tf_op jit(solution)/shard_map/all_to_all | solution.py:461
  17.5 0.0 collective-permute-done.refs_3_
  17.5 0.2 collective-permute-done.1.refs_4_
  17.7 6.7 %fine.1.after_hbm.done_hbm = f32[8,128,512]{2,1,0:T(8,128)} custom-call(s32[1]{0:T(128)} %bitcast.late_ref, s32[56]{0:T(128)} %refs_0_.3, s32[56]{0:T(128)} %refs_1_.3, s32[1]{0:T(128)S(6)} %copy.20.refs_2_, bf16[2,128,512]{2,1,0:T(8,128)(2,1)} %collective-permute-done.refs_3_, bf16[2,128,512]{2,1,0:T(8,128)(2,1)} %collective-permute-done.1.refs_4_, ...), custom_call_target="tpu_custom_call" | custom-call | flops 137438953472 | bytes 1048576 | tf_op jit(solution)/shard_map/fine/pallas_call | solution.py:343
  24.4 1.4 %collective-permute-start.2 = (bf16[2,128,512]{2,1,0:T(8,128)(2,1)}, bf16[2,128,512]{2,1,0:T(8,128)(2,1)}, u32[]{:S(2)}, u32[]{:S(2)}) collective-permute-start(bf16[2,128,512]{2,1,0:T(8,128)(2,1)} %get-tuple-element.14), channel_id=1, source_target_pairs={{64,63},{128,127},{192,191},{256,255},{320,319},{384,383},{448,447}} | collective-permute-start | bytes 786440 | tf_op jit(solution)/shard_map/ppermute | solution.py:466
  25.8 0.1 all-to-all-done.arrived_hbm
  25.9 3.0 %coarse.1.after_hbm = bf16[4,2,16,512]{3,2,1,0:T(8,128)(2,1)} custom-call(s32[1]{0:T(128)} %bitcast.2.sub_ref, s32[2]{0:T(128)} %offset_hbm.1, bf16[16,9,16,128]{3,2,1,0:T(8,128)(2,1)} %all-to-all-done.arrived_hbm, bf16[2,128,128]{2,1,0:T(8,128)(2,1)} %tiles_hbm.1, bf16[1024,512]{1,0:T(8,128)(2,1)} %first_hbm.1, f32[512]{0:T(512)} %bias_hbm.1, ...), custom_call_target="tpu_custom_call" | custom-call | flops 536870912 | bytes 3145728 | tf_op jit(solution)/shard_map/coarse/pallas_call | solution.py:213
  28.8 9.9 %all-to-all-start.1 = ((bf16[4,2,16,512]{3,2,1,0:T(8,128)(2,1)}), bf16[4,2,16,512]{3,2,1,0:T(8,128)(2,1)}, u32[]{:S(2)}, u32[]{:S(2)}) async-start(bf16[4,2,16,512]{3,2,1,0:T(8,128)(2,1)} %coarse.1.after_hbm), calls=%async_computation.1 | async-start | bytes 262144 | tf_op jit(solution)/shard_map/all_to_all | solution.py:478
  38.7 0.0 collective-permute-done.2.refs_4_
  38.8 0.1 late.1.partial_hbm
  38.9 4.5 %all-to-all-done.1.reply_hbm = bf16[4,2,16,512]{3,2,1,0:T(8,128)(2,1)} async-done(((bf16[4,2,16,512]{3,2,1,0:T(8,128)(2,1)}), bf16[4,2,16,512]{3,2,1,0:T(8,128)(2,1)}, u32[]{:S(2)}, u32[]{:S(2)}) %all-to-all-start.1) | async-done | bytes 131104 | tf_op jit(solution)/shard_map/all_to_all | solution.py:478
  43.3 3.0 %finish.1 = bf16[8,128,512]{2,1,0:T(8,128)(2,1)} custom-call(s32[8]{0:T(128)} %owner_hbm.3, f32[8,128,512]{2,1,0:T(8,128)} %late.1.partial_hbm, bf16[4,2,16,512]{3,2,1,0:T(8,128)(2,1)} %all-to-all-done.1.reply_hbm), custom_call_target="tpu_custom_call" | custom-call | flops 33554432 | bytes 4194304 | tf_op jit(solution)/shard_map/finish/pallas_call | solution.py:405
Async XLA Ops:
  3.1 14.4 %collective-permute-start = (bf16[2,128,512]{2,1,0:T(8,128)(2,1)}, bf16[2,128,512]{2,1,0:T(8,128)(2,1)}, u32[]{:S(2)}, u32[]{:S(2)}) collective-permute-start(bf16[2,128,512]{2,1,0:T(8,128)(2,1)} %get-tuple-element.11), channel_id=1, source_target_pairs={{0,1},{1,2},{2,3},{3,4},{4,5},{5,6},{6,7},{7,8},{8,9},{9,10},{10,1... | collective-permute-start | bytes 786440 | tf_op jit(solution)/shard_map/ppermute | solution.py:457
  7.6 10.1 %collective-permute-start.1 = (bf16[2,128,512]{2,1,0:T(8,128)(2,1)}, bf16[2,128,512]{2,1,0:T(8,128)(2,1)}, u32[]{:S(2)}, u32[]{:S(2)}) collective-permute-start(bf16[2,128,512]{2,1,0:T(8,128)(2,1)} %get-tuple-element.14), channel_id=1, source_target_pairs={{1,0},{2,1},{3,2},{4,3},{5,4},{6,5},{7,6},{8,7},{9,8},{10,9},{11,1... | collective-permute-start | bytes 786440 | tf_op jit(solution)/shard_map/ppermute | solution.py:458
  9.5 16.4 %all-to-all-start = ((bf16[16,9,16,128]{3,2,1,0:T(8,128)(2,1)}), bf16[16,9,16,128]{3,2,1,0:T(8,128)(2,1)}, u32[]{:S(2)}, u32[]{:S(2)}) async-start(bf16[16,9,16,128]{3,2,1,0:T(8,128)(2,1)} %get-tuple-element.13), calls=%async_computation | async-start | bytes 1179648 | tf_op jit(solution)/shard_map/all_to_all | solution.py:461
  24.4 14.3 %collective-permute-start.2 = (bf16[2,128,512]{2,1,0:T(8,128)(2,1)}, bf16[2,128,512]{2,1,0:T(8,128)(2,1)}, u32[]{:S(2)}, u32[]{:S(2)}) collective-permute-start(bf16[2,128,512]{2,1,0:T(8,128)(2,1)} %get-tuple-element.14), channel_id=1, source_target_pairs={{64,63},{128,127},{192,191},{256,255},{320,319},{384,383},{448,447}} | collective-permute-start | bytes 786440 | tf_op jit(solution)/shard_map/ppermute | solution.py:466
  28.8 14.5 %all-to-all-start.1 = ((bf16[4,2,16,512]{3,2,1,0:T(8,128)(2,1)}), bf16[4,2,16,512]{3,2,1,0:T(8,128)(2,1)}, u32[]{:S(2)}, u32[]{:S(2)}) async-start(bf16[4,2,16,512]{3,2,1,0:T(8,128)(2,1)} %coarse.1.after_hbm), calls=%async_computation.1 | async-start | bytes 262144 | tf_op jit(solution)/shard_map/all_to_all | solution.py:478

commit v3 on v2

v3 whole, which is shorter than its diff:
```python
import jax
import jax.numpy as jnp
from jax import lax
from jax.experimental import pallas as pl
from jax.experimental.pallas import tpu as pltpu
from jax.sharding import Mesh
from jax.sharding import PartitionSpec as P

POOL = 8
WIN = 4
ROW = 64
DEPTH = 2
SIDE = 2
F32 = jnp.float32
BF16 = jnp.bfloat16

VMEM_SPEC = pl.BlockSpec(memory_space=pltpu.VMEM)
SMEM_SPEC = pl.BlockSpec(memory_space=pltpu.SMEM)
HBM_SPEC = pl.BlockSpec(memory_space=pltpu.HBM)
ANY_SPEC = pl.BlockSpec(memory_space=pl.ANY)


PARAMS = pltpu.CompilerParams(vmem_limit_bytes=32 << 20)


def held_in_hbm(*arrays):
    return [pltpu.with_memory_space_constraint(array, pltpu.HBM) for array in arrays]


def started(pairs, sems):
    copies = [pltpu.make_async_copy(src, dst, sems.at[i]) for i, (src, dst) in enumerate(pairs)]
    for copy in copies:
        copy.start()
    return copies


def owner_slots(owner_ref, count_ref, block_count):
    for d in range(WIN):
        count_ref[d] = 0
    slots = []
    for k in range(block_count):
        d = owner_ref[k] & (WIN - 1)
        r = count_ref[d]
        count_ref[d] = r + 1
        slots.append((d, r))
    return slots


def pack_kernel(
    owner_hbm, halo_hbm, nodes_hbm, send_ref, lower_ref, upper_ref,
    owner_ref, halo_ref, nodes_ref, count_ref, index_ref, int_sems, node_sems,
):
    blocks, rows, width = nodes_ref.shape
    tile = rows // POOL
    lanes = send_ref.shape[-1]
    groups = width // lanes
    subs = send_ref.shape[0] // WIN
    halo = lower_ref.shape[0]
    ints = started([(owner_hbm, owner_ref), (halo_hbm, halo_ref)], int_sems)
    loads = started([(nodes_hbm.at[k], nodes_ref.at[k]) for k in range(blocks)], node_sems)
    row = lax.broadcasted_iota(jnp.int32, (tile, rows), 0)
    col = lax.broadcasted_iota(jnp.int32, (tile, rows), 1)
    average = jnp.where(col // POOL == row, 1.0 / POOL, 0.0).astype(BF16)
    for copy in ints:
        copy.wait()
    slots = owner_slots(owner_ref, count_ref, blocks)
    for k, (d, r) in enumerate(slots):
        index_ref[d * 2 + r] = k
    lane = lax.broadcasted_iota(jnp.int32, (tile, lanes), 1)
    for d in range(WIN):
        tag = jnp.where((lane // tile) % 2 == 0, index_ref[2 * d], index_ref[2 * d + 1])
        tag = tag.astype(F32).astype(BF16)
        for s in range(subs):
            send_ref[d * subs + s, groups * 2] = tag
    for k, (d, r) in enumerate(slots):
        loads[k].wait()
        pooled = jnp.dot(average, nodes_ref[k], preferred_element_type=F32).astype(BF16)
        for s in range(subs):
            for c in range(groups):
                send_ref[d * subs + s, c * 2 + r] = pooled[:, c * lanes : (c + 1) * lanes]
    for h in range(halo):
        lower_ref[h] = nodes_ref[halo_ref[h]]
        upper_ref[h] = nodes_ref[halo_ref[halo + h]]


def pack(pool_owner, halo_blocks, blocks, subs):
    count, rows, width = blocks.shape
    tile = rows // POOL
    halos = halo_blocks.shape[0]
    lanes = 128
    pieces = 2 * (width // lanes) + 1
    return pl.pallas_call(
        pack_kernel,
        name="pack",
        out_shape=(
            jax.ShapeDtypeStruct((WIN * subs, pieces, tile, lanes), BF16),
            jax.ShapeDtypeStruct((halos // 2, rows, width), BF16),
            jax.ShapeDtypeStruct((halos // 2, rows, width), BF16),
        ),
        in_specs=[HBM_SPEC] * 3,
        out_specs=(VMEM_SPEC,) * 3,
        scratch_shapes=[
            pltpu.SMEM((count,), jnp.int32),
            pltpu.SMEM((halos,), jnp.int32),
            pltpu.VMEM(blocks.shape, BF16),
            pltpu.SMEM((WIN,), jnp.int32),
            pltpu.SMEM((2 * WIN,), jnp.int32),
            pltpu.SemaphoreType.DMA((2,)),
            pltpu.SemaphoreType.DMA((count,)),
        ],
        compiler_params=PARAMS,
        cost_estimate=pl.CostEstimate(flops=1 << 27, bytes_accessed=3 << 20, transcendentals=0),
    )(*held_in_hbm(pool_owner, halo_blocks, blocks))


def normalised(values, gain):
    row_mean = jnp.mean(values, axis=-1, keepdims=True)
    centred = values - row_mean
    variance = jnp.mean(centred * centred, axis=-1, keepdims=True)
    return centred * lax.rsqrt(variance + 1e-05) * gain


def network(nodes, messages, first_ref, bias_ref, second_ref, gain_ref):
    width = nodes.shape[1]
    hidden = jnp.dot(nodes, first_ref[:width], preferred_element_type=F32)
    hidden += jnp.dot(messages, first_ref[width:], preferred_element_type=F32)
    hidden = jnp.maximum(hidden + bias_ref[...], 0.0).astype(BF16)
    projected = jnp.dot(hidden, second_ref[...], preferred_element_type=F32)
    return normalised(projected, gain_ref[...])


def coarse_kernel(
    sub_ref, offset_hbm, second_hbm, arrived_ref, tiles_ref, first_ref, bias_ref, gain_ref, reply_ref,
    offset_ref, second_ref, sems,
):
    senders, pieces, tile, lanes = arrived_ref.shape
    groups = pieces // 2
    subs = senders // WIN
    entries, rows, _ = tiles_ref.shape
    loads = started([(offset_hbm, offset_ref), (second_hbm, second_ref)], sems)
    row = lax.broadcasted_iota(jnp.int32, (rows, rows), 0)
    col = lax.broadcasted_iota(jnp.int32, (rows, rows), 1)
    same_row = row % tile == col % tile

    def arrived_rows(s):
        return jnp.concatenate(
            [
                jnp.concatenate([arrived_ref[m * subs + s, c * 2 + r] for c in range(groups)], axis=1)
                for m in range(WIN)
                for r in range(2)
            ],
            axis=0,
        )

    def placing(s):
        tags = jnp.zeros((8, lanes), F32)
        lane = lax.broadcasted_iota(jnp.int32, (8, lanes), 1)
        for m in range(WIN):
            tag = arrived_ref[m * subs + s, groups * 2].astype(F32)[:8]
            tags = jnp.where(lane // (2 * tile) == m, tag, tags)
        return jnp.where(same_row & (row // tile == tags[:1].astype(jnp.int32)), 1.0, 0.0)

    own = sub_ref[0]
    own_rows = arrived_rows(own)
    own_back = placing(own).T.astype(BF16)
    loads[0].wait()
    weights, sources = [], []
    for e in range(entries):
        s = lax.rem(own + offset_ref[e], subs)
        sources.append(arrived_rows(s))
        by_col = jnp.dot(tiles_ref[e], placing(s).astype(BF16), preferred_element_type=F32)
        weights.append(by_col.astype(BF16))
    by_col = jnp.concatenate(weights, axis=1)
    by_both = jnp.dot(own_back, by_col, preferred_element_type=F32).astype(BF16)
    messages = jnp.dot(by_both, jnp.concatenate(sources, axis=0), preferred_element_type=F32)
    loads[1].wait()
    delta = network(own_rows, messages.astype(BF16), first_ref, bias_ref, second_ref, gain_ref)
    delta = delta.astype(BF16)
    for m in range(WIN):
        for r in range(2):
            at = (m * 2 + r) * tile
            reply_ref[m, r] = delta[at : at + tile]


def coarse_update(own_sub, offsets, second, arrived, held):
    return pl.pallas_call(
        coarse_kernel,
        name="coarse",
        out_shape=jax.ShapeDtypeStruct((WIN, 2, arrived.shape[2], second.shape[0]), BF16),
        in_specs=[SMEM_SPEC, HBM_SPEC, HBM_SPEC] + [VMEM_SPEC] * 5,
        out_specs=VMEM_SPEC,
        scratch_shapes=[
            pltpu.SMEM(offsets.shape, jnp.int32),
            pltpu.VMEM(second.shape, BF16),
            pltpu.SemaphoreType.DMA((2,)),
        ],
        compiler_params=PARAMS,
        cost_estimate=pl.CostEstimate(flops=1 << 29, bytes_accessed=3 << 20, transcendentals=0),
    )(own_sub, *held_in_hbm(offsets, second), arrived, *held)


def add_messages(
    target_ref, source_ref, live, table, tiles, total, order, place, loads
):
    blocks = total.shape[0]
    entries = target_ref.shape[0]
    slots = order.shape[0]
    for b in range(blocks + 1):
        place[b] = 0
    for i in range(slots):
        order[i] = entries
    bins = []
    for e in range(entries):
        b = jnp.where(e < live, target_ref[e], blocks)
        place[b] = place[b] + 1
        bins.append(b)
    at = 0
    for b in range(blocks):
        steps = (place[b] + (DEPTH - 1)) // DEPTH
        place[b] = at * DEPTH
        at = at + steps
    place[blocks] = slots - entries
    used = at
    for e in range(entries):
        at = place[bins[e]]
        place[bins[e]] = at + 1
        order[at] = e + (source_ref[e] << 8) + (bins[e] << 16)
    for copy in loads:
        copy.wait()

    @pl.loop(0, (used + (SIDE - 1)) // SIDE)
    def _(i):
        products = []
        for u in range(SIDE):
            codes = [order[(i * SIDE + u) * DEPTH + g] for g in range(DEPTH)]
            left = jnp.concatenate([tiles[code & 255] for code in codes], axis=1)
            right = jnp.concatenate([table[(code >> 8) & 255] for code in codes], axis=0)
            product = jnp.dot(left, right, preferred_element_type=F32)
            products.append((codes[0] >> 16, product))
        for b, product in products:
            total[b] += product


def order_slots(entries, blocks):
    groups = entries // DEPTH + blocks
    return (groups + SIDE - 1) // SIDE * SIDE * DEPTH + entries


def fine_body(
    target_hbm, source_hbm, count_ref, lower_hbm, upper_hbm, edges_hbm, nodes_hbm,
    first_hbm, bias_hbm, second_hbm, gain_hbm,
    target_ref, source_ref, table, tiles, total, order, place,
    first_ref, bias_ref, second_ref, gain_ref, sems, use,
):
    entries = edges_hbm.shape[0]
    halo = lower_hbm.shape[0]
    blocks, rows, width = total.shape
    loads = started(
        [
            (target_hbm, target_ref),
            (source_hbm, source_ref),
            (edges_hbm, tiles.at[pl.ds(0, entries)]),
            (nodes_hbm, table.at[pl.ds(0, blocks)]),
            (lower_hbm, table.at[pl.ds(blocks, halo)]),
            (upper_hbm, table.at[pl.ds(blocks + halo, halo)]),
            (first_hbm, first_ref),
            (second_hbm, second_ref),
            (bias_hbm, bias_ref.at[0]),
            (gain_hbm, gain_ref.at[0]),
        ],
        sems,
    )
    tiles[entries] = jnp.zeros(tiles.shape[1:], BF16)
    total[...] = jnp.zeros_like(total)
    for copy in loads[:2]:
        copy.wait()
    add_messages(target_ref, source_ref, count_ref[0], table, tiles, total, order, place, loads[2:6])
    for copy in loads[6:]:
        copy.wait()
    for i in range(blocks // 2):
        nodes = table[2 * i : 2 * i + 2].reshape(2 * rows, width)
        messages = total[2 * i : 2 * i + 2].reshape(2 * rows, width).astype(BF16)
        use(i, nodes.astype(F32) + network(nodes, messages, first_ref, bias_ref, second_ref, gain_ref))


def fine_scratch(edges, nodes, halo, first, second):
    entries, rows, _ = edges.shape
    blocks, _, width = nodes.shape
    return [
        pltpu.SMEM((entries,), jnp.int32),
        pltpu.SMEM((entries,), jnp.int32),
        pltpu.VMEM((blocks + 2 * halo, rows, width), BF16),
        pltpu.VMEM((entries + 1, rows, rows), BF16),
        pltpu.VMEM(nodes.shape, F32),
        pltpu.SMEM((order_slots(entries, blocks),), jnp.int32),
        pltpu.SMEM((blocks + 1,), jnp.int32),
        pltpu.VMEM(first.shape, BF16),
        pltpu.VMEM((1, width), F32),
        pltpu.VMEM(second.shape, BF16),
        pltpu.VMEM((1, width), F32),
        pltpu.SemaphoreType.DMA((10,)),
    ]


FINE_SPECS = [HBM_SPEC, HBM_SPEC, SMEM_SPEC, ANY_SPEC, ANY_SPEC] + [HBM_SPEC] * 6


def fine_inputs(entries, lower, upper, edges, nodes, first, bias, second, gain):
    target, source, count = entries
    return [
        *held_in_hbm(target, source),
        count,
        lower,
        upper,
        *held_in_hbm(edges, nodes, first, bias, second, gain),
    ]


def fine_kernel(late_ref, owner_hbm, *refs):
    coarse_hbm, fine_in, outs, scratch = refs[:4], refs[4:15], refs[15:21], refs[21:]
    partial_ref, slot_ref, *coarse_refs = outs
    *fine_refs, owner_ref, count_ref, sems = scratch
    blocks, rows, width = partial_ref.shape
    tile = rows // POOL
    loads = started(
        [(owner_hbm, owner_ref)]
        + [
            (src, dst.at[0] if dst.shape != src.shape else dst)
            for src, dst in zip(coarse_hbm, coarse_refs)
        ],
        sems,
    )
    loads[0].wait()
    for k, (d, r) in enumerate(owner_slots(owner_ref, count_ref, blocks)):
        slot_ref[k] = jnp.full(slot_ref.shape[1:], (d * 2 + r) * tile, jnp.int32)

    @pl.when(late_ref[0] == 0)
    def _():
        def use(i, values):
            partial_ref[2 * i : 2 * i + 2] = values.astype(BF16).reshape(2, rows, width)

        fine_body(*fine_in, *fine_refs, use)

    for copy in loads[1:]:
        copy.wait()


def fine_update(late, pool_owner, coarse, fine_in):
    edges, nodes, first, _, second, _ = fine_in[5:]
    blocks, rows, width = nodes.shape
    tiles, coarse_first, _, _ = coarse
    partial, slots, *held = pl.pallas_call(
        fine_kernel,
        name="fine",
        out_shape=(
            jax.ShapeDtypeStruct(nodes.shape, BF16),
            jax.ShapeDtypeStruct((blocks, 8, rows), jnp.int32),
            jax.ShapeDtypeStruct(tiles.shape, BF16),
            jax.ShapeDtypeStruct(coarse_first.shape, BF16),
            jax.ShapeDtypeStruct((1, width), F32),
            jax.ShapeDtypeStruct((1, width), F32),
        ),
        in_specs=[SMEM_SPEC] + [HBM_SPEC] * 5 + FINE_SPECS,
        out_specs=(VMEM_SPEC,) * 6,
        scratch_shapes=fine_scratch(edges, nodes, fine_in[3].shape[0], first, second)
        + [pltpu.SMEM((blocks,), jnp.int32), pltpu.SMEM((WIN,), jnp.int32), pltpu.SemaphoreType.DMA((5,))],
        compiler_params=PARAMS,
        cost_estimate=pl.CostEstimate(flops=1 << 37, bytes_accessed=1 << 20, transcendentals=0),
    )(late, *held_in_hbm(pool_owner, *coarse), *fine_in)
    return partial, slots, held


def finish_kernel(late_ref, partial_ref, slot_ref, reply_ref, *refs):
    fine_in, out_hbm, (*fine_refs, out_ref, out_sems) = refs[:11], refs[11], refs[12:]
    blocks, rows, width = partial_ref.shape
    row = lax.broadcasted_iota(jnp.int32, (rows, rows), 0)
    col = lax.broadcasted_iota(jnp.int32, (rows, rows), 1)
    place = col - row // POOL

    def use(i, values):
        at = pl.ds(2 * i, 2)
        spread = [jnp.where(place == slot_ref[k][:1], 1.0, 0.0) for k in (2 * i, 2 * i + 1)]
        spread = jnp.concatenate(spread, axis=0).astype(BF16)
        back = jnp.dot(spread, reply_ref[...].reshape(rows, width), preferred_element_type=F32)
        out_ref[2 * i : 2 * i + 2] = (values + back).astype(BF16).reshape(2, rows, width)
        started([(out_ref.at[at], out_hbm.at[at])], out_sems.at[pl.ds(i, 1)])

    @pl.when(late_ref[0] == 0)
    def _():
        for i in range(blocks // 2):
            use(i, partial_ref[2 * i : 2 * i + 2].reshape(2 * rows, width).astype(F32))

    @pl.when(late_ref[0] == 1)
    def _():
        fine_body(*fine_in, *fine_refs, use)

    for i in range(blocks // 2):
        at = pl.ds(2 * i, 2)
        pltpu.make_async_copy(out_ref.at[at], out_hbm.at[at], out_sems.at[i]).wait()


def finish(late, partial, slots, reply, fine_in):
    edges, nodes, first, _, second, _ = fine_in[5:]
    return pl.pallas_call(
        finish_kernel,
        name="finish",
        out_shape=jax.ShapeDtypeStruct(partial.shape, BF16),
        in_specs=[SMEM_SPEC] + [VMEM_SPEC] * 3 + FINE_SPECS,
        out_specs=ANY_SPEC,
        scratch_shapes=fine_scratch(edges, nodes, fine_in[3].shape[0], first, second)
        + [pltpu.VMEM(partial.shape, BF16), pltpu.SemaphoreType.DMA((partial.shape[0] // 2,))],
        compiler_params=PARAMS,
        cost_estimate=pl.CostEstimate(flops=1 << 25, bytes_accessed=4 << 20, transcendentals=0),
    )(late, partial, slots, reply, *fine_in)


def per_device(
    fine_nodes,
    edge_tiles,
    edge_target,
    edge_source,
    edge_count,
    halo_blocks,
    pool_owner,
    coarse_tiles,
    pooled_block_source_index,
    fine_first,
    fine_bias,
    fine_second,
    fine_gain,
    coarse_first,
    coarse_bias,
    coarse_second,
    pooled_level_scale_factor,
):
    block_count = pool_owner.shape[0]
    rows = edge_tiles.shape[1]
    width = fine_nodes.shape[1]
    subs = lax.axis_size("sub")
    everyone = ("win", "mem", "sub")
    devices = lax.axis_size(everyone)
    blocks = fine_nodes.reshape(block_count, rows, width)

    own_sub = lax.axis_index("sub").astype(jnp.int32)[None]
    index = lax.axis_index(everyone)
    late = ((index % ROW == ROW - 1) & (index < devices - 1)).astype(jnp.int32)[None]
    send, lower, upper = pack(pool_owner, halo_blocks, blocks, subs)
    from_lower = lax.ppermute(upper, everyone, [(i, i + 1) for i in range(devices - 1)])
    from_upper = lax.ppermute(
        lower, everyone, [(i + 1, i) for i in range(devices - 1) if (i + 1) % ROW]
    )
    arrived = lax.all_to_all(send, ("mem", "sub"), 0, 0, tiled=True)
    entries = (edge_target, edge_source, edge_count)
    network_in = (edge_tiles, blocks, fine_first, fine_bias, fine_second, fine_gain)
    coarse_in = (coarse_tiles, coarse_first, coarse_bias, pooled_level_scale_factor)
    partial, slots, held = fine_update(
        late, pool_owner, coarse_in, fine_inputs(entries, from_lower, from_upper, *network_in)
    )
    lower, partial = lax.optimization_barrier((lower, partial))
    late_upper = lax.ppermute(lower, everyone, [(i, i - 1) for i in range(ROW, devices, ROW)])
    reply = coarse_update(own_sub, pooled_block_source_index, coarse_second, arrived, held)
    returned = lax.all_to_all(reply, "mem", 0, 0, tiled=True)
    late_in = fine_inputs(entries, from_lower, late_upper, *network_in)
    return finish(late, partial, slots, returned, late_in).reshape(fine_nodes.shape)


def solution(mesh):
    dom, sub = mesh.devices.shape
    split = Mesh(mesh.devices.reshape(dom // WIN, WIN, sub), ("win", "mem", "sub"))
    every = ("win", "mem", "sub")
    placed = (
        P(every, None),
        P(every, None, None),
        P(every),
        P(every),
        P(every),
        P(every),
        P(every),
        P(every, None, None),
        P(every),
        P(),
        P(),
        P(),
        P(),
        P(),
        P(),
        P(),
        P(),
    )
    return jax.shard_map(
        per_device, mesh=split, in_specs=placed, out_specs=P(every, None), check_vma=False
    )
```

time: 46.7 us -> 43.1 us (0.923)
  the two profiles are of different devices: /device:TPU:191 before, /device:TPU:495 now
where the time goes in v3:
time: 43.1 us; the launch traced here: 42.7 us
  starting transfers between devices  18.5 us (43%)
  Pallas kernels  15.6 us (36%)
  waiting for transfers between devices  7.88 us (18%)
  between operations  0.72 us (2%)
    pallas_call x1, Pallas kernels, finish(): pl.pallas_call(finish_kernel, name='finish', out_shape=jax.ShapeDtypeStru...  8.8 us
    all_to_all x1, starting transfers between devices, per_device(): arrived = lax.all_to_all(send, ('mem', 'sub'), 0, 0, tiled=True)  6.62 us
    all_to_all x1, starting transfers between devices, per_device(): returned = lax.all_to_all(reply, 'mem', 0, 0, tiled=True)  5.25 us
    all_to_all x1, waiting for transfers between devices, per_device(): arrived = lax.all_to_all(send, ('mem', 'sub'), 0, 0, tiled=True)  5.15 us
    ppermute x1, starting transfers between devices, per_device(): lax.ppermute(lower, everyone, [(i + 1, i) for i in range(devices - 1) if...  3.37 us
    pallas_call x1, Pallas kernels, pack(): pl.pallas_call(pack_kernel, name='pack', out_shape=(jax.ShapeDtypeStruct(...  2.93 us
    all_to_all x1, waiting for transfers between devices, per_device(): returned = lax.all_to_all(reply, 'mem', 0, 0, tiled=True)  2.72 us
    pallas_call x1, Pallas kernels, coarse_update(): pl.pallas_call(coarse_kernel, name='coarse', out_shape=jax.ShapeDtypeStru...  2.46 us
  transfers between devices with their start and end apart: 5, of which 2 were waited for; matrix products, arithmetic and copies ran while one was open for 0% of the time, Pallas kernels for 9%

profile of v3, /device:TPU:495, one launch (start us, length us, event | category | flops | bytes accessed | tf_op | source)
XLA Modules:
  0.0 42.7 jit_solution(11454000868307312458)
XLA Ops:
  0.0 2.9 %pack.1 = (bf16[16,9,16,128]{3,2,1,0:T(8,128)(2,1)}, bf16[2,128,512]{2,1,0:T(8,128)(2,1)}, bf16[2,128,512]{2,1,0:T(8,128)(2,1)S(1)}) custom-call(s32[8]{0:T(128)} %owner_hbm.3, s32[4]{0:T(128)} %halo_hbm.1, bf16[8,128,512]{2,1,0:T(8,128)(2,1)} %bitcast.4), custom_call_target="tpu_custom_call" | custom-call | flops 134217728 | bytes 3145728 | tf_op jit(solution)/shard_map/pack/pallas_call | solution.py:92
  2.9 1.9 %collective-permute-start = (bf16[2,128,512]{2,1,0:T(8,128)(2,1)S(1)}, bf16[2,128,512]{2,1,0:T(8,128)(2,1)S(1)}, u32[]{:S(2)}, u32[]{:S(2)}) collective-permute-start(bf16[2,128,512]{2,1,0:T(8,128)(2,1)S(1)} %get-tuple-element.17), channel_id=1, source_target_pairs={{0,1},{1,2},{2,3},{3,4},{4,5},{5,6},{6,7},{7,8},{8,9},{9,10},{10,1... | collective-permute-start | bytes 786440 | tf_op jit(solution)/shard_map/ppermute | solution.py:448
  4.9 3.4 %collective-permute-start.1 = (bf16[2,128,512]{2,1,0:T(8,128)(2,1)}, bf16[2,128,512]{2,1,0:T(8,128)(2,1)S(1)}, u32[]{:S(2)}, u32[]{:S(2)}) collective-permute-start(bf16[2,128,512]{2,1,0:T(8,128)(2,1)} %get-tuple-element.26), channel_id=1, source_target_pairs={{1,0},{2,1},{3,2},{4,3},{5,4},{6,5},{7,6},{8,7},{9,8},{10,9},{11,1... | collective-permute-start | bytes 786440 | tf_op jit(solution)/shard_map/ppermute | solution.py:449
  8.2 6.6 %all-to-all-start = ((bf16[16,9,16,128]{3,2,1,0:T(8,128)(2,1)}), bf16[16,9,16,128]{3,2,1,0:T(8,128)(2,1)S(1)}, u32[]{:S(2)}, u32[]{:S(2)}) async-start(bf16[16,9,16,128]{3,2,1,0:T(8,128)(2,1)} %get-tuple-element.21), calls=%async_computation | async-start | bytes 1179648 | tf_op jit(solution)/shard_map/all_to_all | solution.py:452
  15.5 0.0 collective-permute-done.refs_7_.refs_3_
  15.5 0.0 collective-permute-done.1.refs_8_
  15.5 1.4 %fine.1 = (bf16[8,128,512]{2,1,0:T(8,128)(2,1)S(1)}, s32[8,8,128]{2,1,0:T(8,128)S(1)}, bf16[2,128,128]{2,1,0:T(8,128)(2,1)S(1)}, bf16[1024,512]{1,0:T(8,128)(2,1...) custom-call(s32[1]{0:T(128)} %bitcast.late_ref, s32[8]{0:T(128)} %owner_hbm.3, bf16[2,128,128]{2,1,0:T(8,128)(2,1)} %refs_0_.2, ...), custom_call_target="tpu_custom_call" | custom-call | flops 137438953472 | bytes 1048576 | tf_op jit(solution)/shard_map/fine/pallas_call | solution.py:352
  17.0 1.3 %collective-permute-start.2 = (bf16[2,128,512]{2,1,0:T(8,128)(2,1)}, bf16[2,128,512]{2,1,0:T(8,128)(2,1)S(1)}, u32[]{:S(2)}, u32[]{:S(2)}) collective-permute-start(bf16[2,128,512]{2,1,0:T(8,128)(2,1)} %get-tuple-element.26), channel_id=1, source_target_pairs={{64,63},{128,127},{192,191},{256,255},{320,319},{384,383},{448,447}} | collective-permute-start | bytes 786440 | tf_op jit(solution)/shard_map/ppermute | solution.py:460
  18.3 5.2 %all-to-all-done.arrived_ref = bf16[16,9,16,128]{3,2,1,0:T(8,128)(2,1)S(1)} async-done(((bf16[16,9,16,128]{3,2,1,0:T(8,128)(2,1)}), bf16[16,9,16,128]{3,2,1,0:T(8,128)(2,1)S(1)}, u32[]{:S(2)}, u32[]{:S(2)}) %all-to-all-start) | async-done | bytes 589856 | tf_op jit(solution)/shard_map/all_to_all | solution.py:452
  23.4 2.5 %coarse.1 = bf16[4,2,16,512]{3,2,1,0:T(8,128)(2,1)} custom-call(s32[1]{0:T(128)} %bitcast.2.sub_ref, s32[2]{0:T(128)} %offset_hbm.1, bf16[512,512]{1,0:T(8,128)(2,1)} %second_hbm.1, bf16[16,9,16,128]{3,2,1,0:T(8,128)(2,1)S(1)} %all-to-all-done.arrived_ref, bf16[2,128,128]{2,1,0:T(8,128)(2,1)S(1)} %get-tuple-element.22.tiles_ref, ...), custom_call_target="tpu_custom_call" | custom-call | flops 536870912 | bytes 3145728 | tf_op jit(solution)/shard_map/coarse/pallas_call | solution.py:186
  25.9 5.2 %all-to-all-start.1 = ((bf16[4,2,16,512]{3,2,1,0:T(8,128)(2,1)}), bf16[4,2,16,512]{3,2,1,0:T(8,128)(2,1)S(1)}, u32[]{:S(2)}, u32[]{:S(2)}) async-start(bf16[4,2,16,512]{3,2,1,0:T(8,128)(2,1)} %coarse.1), calls=%async_computation.1 | async-start | bytes 262144 | tf_op jit(solution)/shard_map/all_to_all | solution.py:462
  31.1 0.0 collective-permute-done.2.refs_4_
  31.1 2.7 %all-to-all-done.1.reply_ref = bf16[4,2,16,512]{3,2,1,0:T(8,128)(2,1)S(1)} async-done(((bf16[4,2,16,512]{3,2,1,0:T(8,128)(2,1)}), bf16[4,2,16,512]{3,2,1,0:T(8,128)(2,1)S(1)}, u32[]{:S(2)}, u32[]{:S(2)}) %all-to-all-start.1) | async-done | bytes 131104 | tf_op jit(solution)/shard_map/all_to_all | solution.py:462
  33.9 8.8 %finish.1 = bf16[8,128,512]{2,1,0:T(8,128)(2,1)} custom-call(s32[1]{0:T(128)} %bitcast.late_ref, bf16[8,128,512]{2,1,0:T(8,128)(2,1)S(1)} %get-tuple-element.19.partial_ref, s32[8,8,128]{2,1,0:T(8,128)S(1)} %get-tuple-element.20.slot_ref, bf16[4,2,16,512]{3,2,1,0:T(8,128)(2,1)S(1)} %all-to-all-done.1.reply_ref, s32[56]{0:T(128)} %refs_0_.3, s32[56]{0:T(128)} %refs_1_.3, ...), custom_call_target="tpu_custom_call" | custom-call | flops 33554432 | bytes 4194304 | tf_op jit(solution)/shard_map/finish/pallas_call | solution.py:404
Async XLA Ops:
  2.9 12.6 %collective-permute-start = (bf16[2,128,512]{2,1,0:T(8,128)(2,1)S(1)}, bf16[2,128,512]{2,1,0:T(8,128)(2,1)S(1)}, u32[]{:S(2)}, u32[]{:S(2)}) collective-permute-start(bf16[2,128,512]{2,1,0:T(8,128)(2,1)S(1)} %get-tuple-element.17), channel_id=1, source_target_pairs={{0,1},{1,2},{2,3},{3,4},{4,5},{5,6},{6,7},{7,8},{8,9},{9,10},{10,1... | collective-permute-start | bytes 786440 | tf_op jit(solution)/shard_map/ppermute | solution.py:448
  4.9 10.7 %collective-permute-start.1 = (bf16[2,128,512]{2,1,0:T(8,128)(2,1)}, bf16[2,128,512]{2,1,0:T(8,128)(2,1)S(1)}, u32[]{:S(2)}, u32[]{:S(2)}) collective-permute-start(bf16[2,128,512]{2,1,0:T(8,128)(2,1)} %get-tuple-element.26), channel_id=1, source_target_pairs={{1,0},{2,1},{3,2},{4,3},{5,4},{6,5},{7,6},{8,7},{9,8},{10,9},{11,1... | collective-permute-start | bytes 786440 | tf_op jit(solution)/shard_map/ppermute | solution.py:449
  8.2 15.2 %all-to-all-start = ((bf16[16,9,16,128]{3,2,1,0:T(8,128)(2,1)}), bf16[16,9,16,128]{3,2,1,0:T(8,128)(2,1)S(1)}, u32[]{:S(2)}, u32[]{:S(2)}) async-start(bf16[16,9,16,128]{3,2,1,0:T(8,128)(2,1)} %get-tuple-element.21), calls=%async_computation | async-start | bytes 1179648 | tf_op jit(solution)/shard_map/all_to_all | solution.py:452
  17.0 14.2 %collective-permute-start.2 = (bf16[2,128,512]{2,1,0:T(8,128)(2,1)}, bf16[2,128,512]{2,1,0:T(8,128)(2,1)S(1)}, u32[]{:S(2)}, u32[]{:S(2)}) collective-permute-start(bf16[2,128,512]{2,1,0:T(8,128)(2,1)} %get-tuple-element.26), channel_id=1, source_target_pairs={{64,63},{128,127},{192,191},{256,255},{320,319},{384,383},{448,447}} | collective-permute-start | bytes 786440 | tf_op jit(solution)/shard_map/ppermute | solution.py:460
  25.9 8.0 %all-to-all-start.1 = ((bf16[4,2,16,512]{3,2,1,0:T(8,128)(2,1)}), bf16[4,2,16,512]{3,2,1,0:T(8,128)(2,1)S(1)}, u32[]{:S(2)}, u32[]{:S(2)}) async-start(bf16[4,2,16,512]{3,2,1,0:T(8,128)(2,1)} %coarse.1), calls=%async_computation.1 | async-start | bytes 262144 | tf_op jit(solution)/shard_map/all_to_all | solution.py:462

commit v4 on v3

--- a/solution.py
+++ b/solution.py
@@ -10,7 +10,7 @@
 WIN = 4
 ROW = 64
 DEPTH = 2
-SIDE = 2
+SIDE = 4
 F32 = jnp.float32
 BF16 = jnp.bfloat16
 
@@ -47,8 +47,9 @@
 
 
 def pack_kernel(
-    owner_hbm, halo_hbm, nodes_hbm, send_ref, lower_ref, upper_ref,
-    owner_ref, halo_ref, nodes_ref, count_ref, index_ref, int_sems, node_sems,
+    owner_hbm, halo_hbm, nodes_hbm, first_hbm, tiles_hbm, bias_hbm, gain_hbm,
+    send_ref, lower_ref, upper_ref, slot_ref, first_ref, tiles_ref, bias_ref, gain_ref,
+    owner_ref, halo_ref, nodes_ref, count_ref, index_ref, int_sems, node_sems, held_sems,
 ):
     blocks, rows, width = nodes_ref.shape
     tile = rows // POOL
@@ -58,6 +59,15 @@
     halo = lower_ref.shape[0]
     ints = started([(owner_hbm, owner_ref), (halo_hbm, halo_ref)], int_sems)
     loads = started([(nodes_hbm.at[k], nodes_ref.at[k]) for k in range(blocks)], node_sems)
+    held = started(
+        [
+            (first_hbm, first_ref),
+            (tiles_hbm, tiles_ref),
+            (bias_hbm, bias_ref.at[0]),
+            (gain_hbm, gain_ref.at[0]),
+        ],
+        held_sems,
+    )
     row = lax.broadcasted_iota(jnp.int32, (tile, rows), 0)
     col = lax.broadcasted_iota(jnp.int32, (tile, rows), 1)
     average = jnp.where(col // POOL == row, 1.0 / POOL, 0.0).astype(BF16)
@@ -66,6 +76,7 @@
     slots = owner_slots(owner_ref, count_ref, blocks)
     for k, (d, r) in enumerate(slots):
         index_ref[d * 2 + r] = k
+        slot_ref[k] = jnp.full(slot_ref.shape[1:], (d * 2 + r) * tile, jnp.int32)
     lane = lax.broadcasted_iota(jnp.int32, (tile, lanes), 1)
     for d in range(WIN):
         tag = jnp.where((lane // tile) % 2 == 0, index_ref[2 * d], index_ref[2 * d + 1])
@@ -81,9 +92,11 @@
     for h in range(halo):
         lower_ref[h] = nodes_ref[halo_ref[h]]
         upper_ref[h] = nodes_ref[halo_ref[halo + h]]
-
-
-def pack(pool_owner, halo_blocks, blocks, subs):
+    for copy in held:
+        copy.wait()
+
+
+def pack(pool_owner, halo_blocks, blocks, first, tiles, bias, gain, subs):
     count, rows, width = blocks.shape
     tile = rows // POOL
     halos = halo_blocks.shape[0]
@@ -96,9 +109,14 @@
             jax.ShapeDtypeStruct((WIN * subs, pieces, tile, lanes), BF16),
             jax.ShapeDtypeStruct((halos // 2, rows, width), BF16),
             jax.ShapeDtypeStruct((halos // 2, rows, width), BF16),
+            jax.ShapeDtypeStruct((count, 8, rows), jnp.int32),
+            jax.ShapeDtypeStruct(first.shape, BF16),
+            jax.ShapeDtypeStruct(tiles.shape, BF16),
+            jax.ShapeDtypeStruct((1, width), F32),
+            jax.ShapeDtypeStruct((1, width), F32),
         ),
-        in_specs=[HBM_SPEC] * 3,
-        out_specs=(VMEM_SPEC,) * 3,
+        in_specs=[HBM_SPEC] * 7,
+        out_specs=(VMEM_SPEC,) * 8,
         scratch_shapes=[
             pltpu.SMEM((count,), jnp.int32),
             pltpu.SMEM((halos,), jnp.int32),
@@ -107,10 +125,11 @@
             pltpu.SMEM((2 * WIN,), jnp.int32),
             pltpu.SemaphoreType.DMA((2,)),
             pltpu.SemaphoreType.DMA((count,)),
+            pltpu.SemaphoreType.DMA((4,)),
         ],
         compiler_params=PARAMS,
         cost_estimate=pl.CostEstimate(flops=1 << 27, bytes_accessed=3 << 20, transcendentals=0),
-    )(*held_in_hbm(pool_owner, halo_blocks, blocks))
+    )(*held_in_hbm(pool_owner, halo_blocks, blocks, first, tiles, bias, gain))
 
 
 def normalised(values, gain):
@@ -130,7 +149,7 @@
 
 
 def coarse_kernel(
-    sub_ref, offset_hbm, second_hbm, arrived_ref, tiles_ref, first_ref, bias_ref, gain_ref, reply_ref,
+    sub_ref, offset_hbm, second_hbm, arrived_ref, first_ref, tiles_ref, bias_ref, gain_ref, reply_ref,
     offset_ref, second_ref, sems,
 ):
     senders, pieces, tile, lanes = arrived_ref.shape
@@ -316,72 +335,46 @@
     ]
 
 
-def fine_kernel(late_ref, owner_hbm, *refs):
-    coarse_hbm, fine_in, outs, scratch = refs[:4], refs[4:15], refs[15:21], refs[21:]
-    partial_ref, slot_ref, *coarse_refs = outs
-    *fine_refs, owner_ref, count_ref, sems = scratch
-    blocks, rows, width = partial_ref.shape
-    tile = rows // POOL
-    loads = started(
-        [(owner_hbm, owner_ref)]
-        + [
-            (src, dst.at[0] if dst.shape != src.shape else dst)
-            for src, dst in zip(coarse_hbm, coarse_refs)
-        ],
-        sems,
-    )
-    loads[0].wait()
-    for k, (d, r) in enumerate(owner_slots(owner_ref, count_ref, blocks)):
-        slot_ref[k] = jnp.full(slot_ref.shape[1:], (d * 2 + r) * tile, jnp.int32)
+def fine_kernel(late_ref, *refs):
+    fine_in, partial_ref, fine_refs = refs[:11], refs[11], refs[12:]
+    _, rows, width = partial_ref.shape
+
+    def use(i, values):
+        partial_ref[2 * i : 2 * i + 2] = values.astype(BF16).reshape(2, rows, width)
 
     @pl.when(late_ref[0] == 0)
     def _():
-        def use(i, values):
-            partial_ref[2 * i : 2 * i + 2] = values.astype(BF16).reshape(2, rows, width)
-
         fine_body(*fine_in, *fine_refs, use)
 
-    for copy in loads[1:]:
-        copy.wait()
-
-
-def fine_update(late, pool_owner, coarse, fine_in):
+
+def fine_update(late, fine_in):
     edges, nodes, first, _, second, _ = fine_in[5:]
-    blocks, rows, width = nodes.shape
-    tiles, coarse_first, _, _ = coarse
-    partial, slots, *held = pl.pallas_call(
+    return pl.pallas_call(
         fine_kernel,
         name="fine",
-        out_shape=(
-            jax.ShapeDtypeStruct(nodes.shape, BF16),
-            jax.ShapeDtypeStruct((blocks, 8, rows), jnp.int32),
-            jax.ShapeDtypeStruct(tiles.shape, BF16),
-            jax.ShapeDtypeStruct(coarse_first.shape, BF16),
-            jax.ShapeDtypeStruct((1, width), F32),
-            jax.ShapeDtypeStruct((1, width), F32),
-        ),
-        in_specs=[SMEM_SPEC] + [HBM_SPEC] * 5 + FINE_SPECS,
-        out_specs=(VMEM_SPEC,) * 6,
-        scratch_shapes=fine_scratch(edges, nodes, fine_in[3].shape[0], first, second)
-        + [pltpu.SMEM((blocks,), jnp.int32), pltpu.SMEM((WIN,), jnp.int32), pltpu.SemaphoreType.DMA((5,))],
+        out_shape=jax.ShapeDtypeStruct(nodes.shape, BF16),
+        in_specs=[SMEM_SPEC] + FINE_SPECS,
+        out_specs=VMEM_SPEC,
+        scratch_shapes=fine_scratch(edges, nodes, fine_in[3].shape[0], first, second),
         compiler_params=PARAMS,
         cost_estimate=pl.CostEstimate(flops=1 << 37, bytes_accessed=1 << 20, transcendentals=0),
-    )(late, *held_in_hbm(pool_owner, *coarse), *fine_in)
-    return partial, slots, held
-
-
-def finish_kernel(late_ref, partial_ref, slot_ref, reply_ref, *refs):
+    )(late, *fine_in)
+
+
+def finish_kernel(late_ref, mem_ref, partial_ref, slot_ref, replies_ref, *refs):
     fine_in, out_hbm, (*fine_refs, out_ref, out_sems) = refs[:11], refs[11], refs[12:]
     blocks, rows, width = partial_ref.shape
     row = lax.broadcasted_iota(jnp.int32, (rows, rows), 0)
     col = lax.broadcasted_iota(jnp.int32, (rows, rows), 1)
     place = col - row // POOL
+    mine = [replies_ref[q, mem_ref[0]].reshape(rows // WIN, width) for q in range(WIN)]
+    reply = jnp.concatenate(mine, axis=0)
 
     def use(i, values):
         at = pl.ds(2 * i, 2)
         spread = [jnp.where(place == slot_ref[k][:1], 1.0, 0.0) for k in (2 * i, 2 * i + 1)]
         spread = jnp.concatenate(spread, axis=0).astype(BF16)
-        back = jnp.dot(spread, reply_ref[...].reshape(rows, width), preferred_element_type=F32)
+        back = jnp.dot(spread, reply, preferred_element_type=F32)
         out_ref[2 * i : 2 * i + 2] = (values + back).astype(BF16).reshape(2, rows, width)
         started([(out_ref.at[at], out_hbm.at[at])], out_sems.at[pl.ds(i, 1)])
 
@@ -399,19 +392,19 @@
         pltpu.make_async_copy(out_ref.at[at], out_hbm.at[at], out_sems.at[i]).wait()
 
 
-def finish(late, partial, slots, reply, fine_in):
+def finish(late, own_mem, partial, slots, replies, fine_in):
     edges, nodes, first, _, second, _ = fine_in[5:]
     return pl.pallas_call(
         finish_kernel,
         name="finish",
         out_shape=jax.ShapeDtypeStruct(partial.shape, BF16),
-        in_specs=[SMEM_SPEC] + [VMEM_SPEC] * 3 + FINE_SPECS,
+        in_specs=[SMEM_SPEC] * 2 + [VMEM_SPEC] * 3 + FINE_SPECS,
         out_specs=ANY_SPEC,
         scratch_shapes=fine_scratch(edges, nodes, fine_in[3].shape[0], first, second)
         + [pltpu.VMEM(partial.shape, BF16), pltpu.SemaphoreType.DMA((partial.shape[0] // 2,))],
         compiler_params=PARAMS,
         cost_estimate=pl.CostEstimate(flops=1 << 25, bytes_accessed=4 << 20, transcendentals=0),
-    )(late, partial, slots, reply, *fine_in)
+    )(late, own_mem, partial, slots, replies, *fine_in)
 
 
 def per_device(
@@ -444,7 +437,16 @@
     own_sub = lax.axis_index("sub").astype(jnp.int32)[None]
     index = lax.axis_index(everyone)
     late = ((index % ROW == ROW - 1) & (index < devices - 1)).astype(jnp.int32)[None]
-    send, lower, upper = pack(pool_owner, halo_blocks, blocks, subs)
+    send, lower, upper, slots, *held = pack(
+        pool_owner,
+        halo_blocks,
+        blocks,
+        coarse_first,
+        coarse_tiles,
+        coarse_bias,
+        pooled_level_scale_factor,
+        subs,
+    )
     from_lower = lax.ppermute(upper, everyone, [(i, i + 1) for i in range(devices - 1)])
     from_upper = lax.ppermute(
         lower, everyone, [(i + 1, i) for i in range(devices - 1) if (i + 1) % ROW]
@@ -452,16 +454,14 @@
     arrived = lax.all_to_all(send, ("mem", "sub"), 0, 0, tiled=True)
     entries = (edge_target, edge_source, edge_count)
     network_in = (edge_tiles, blocks, fine_first, fine_bias, fine_second, fine_gain)
-    coarse_in = (coarse_tiles, coarse_first, coarse_bias, pooled_level_scale_factor)
-    partial, slots, held = fine_update(
-        late, pool_owner, coarse_in, fine_inputs(entries, from_lower, from_upper, *network_in)
-    )
+    partial = fine_update(late, fine_inputs(entries, from_lower, from_upper, *network_in))
     lower, partial = lax.optimization_barrier((lower, partial))
     late_upper = lax.ppermute(lower, everyone, [(i, i - 1) for i in range(ROW, devices, ROW)])
     reply = coarse_update(own_sub, pooled_block_source_index, coarse_second, arrived, held)
-    returned = lax.all_to_all(reply, "mem", 0, 0, tiled=True)
+    replies = lax.all_gather(reply, "mem")
+    own_mem = lax.axis_index("mem").astype(jnp.int32)[None]
     late_in = fine_inputs(entries, from_lower, late_upper, *network_in)
-    return finish(late, partial, slots, returned, late_in).reshape(fine_nodes.shape)
+    return finish(late, own_mem, partial, slots, replies, late_in).reshape(fine_nodes.shape)
 
 
 def solution(mesh):

time: 43.1 us -> 39.6 us (0.919)
  the two profiles are of different devices: /device:TPU:495 before, /device:TPU:41 now
where the time goes in v4:
time: 39.6 us; the launch traced here: 39.3 us
  starting transfers between devices  13.3 us (34%)
  Pallas kernels  11.3 us (29%)
  blocking collectives  9.17 us (23%)
  waiting for transfers between devices  4.81 us (12%)
  between operations  0.72 us (2%)
    all_gather x1, blocking collectives, per_device(): replies = lax.all_gather(reply, 'mem')  9.17 us
    all_to_all x1, starting transfers between devices, per_device(): arrived = lax.all_to_all(send, ('mem', 'sub'), 0, 0, tiled=True)  5.78 us
    pallas_call x1, Pallas kernels, fine_update(): pl.pallas_call(fine_kernel, name='fine', out_shape=jax.ShapeDtypeStruct(n...  5.13 us
    all_to_all x1, waiting for transfers between devices, per_device(): arrived = lax.all_to_all(send, ('mem', 'sub'), 0, 0, tiled=True)  4.8 us
    ppermute x1, starting transfers between devices, per_device(): lax.ppermute(lower, everyone, [(i + 1, i) for i in range(devices - 1) if...  3.75 us
    ppermute x1, starting transfers between devices, per_device(): lax.ppermute(upper, everyone, [(i, i + 1) for i in range(devices - 1)])  3.12 us
    pallas_call x1, Pallas kernels, pack(): pl.pallas_call(pack_kernel, name='pack', out_shape=(jax.ShapeDtypeStruct(...  3.06 us
    pallas_call x1, Pallas kernels, coarse_update(): pl.pallas_call(coarse_kernel, name='coarse', out_shape=jax.ShapeDtypeStru...  1.8 us
  transfers between devices with their start and end apart: 4, of which 1 were waited for; matrix products, arithmetic and copies ran while one was open for 0% of the time, Pallas kernels for 18%

profile of v4, /device:TPU:41, one launch (start us, length us, event | category | flops | bytes accessed | tf_op | source)
XLA Modules:
  0.0 39.3 jit_solution(5964831031250625862)
XLA Ops:
  0.0 3.1 %pack.1 = (bf16[16,9,16,128]{3,2,1,0:T(8,128)(2,1)}, bf16[2,128,512]{2,1,0:T(8,128)(2,1)}, bf16[2,128,512]{2,1,0:T(8,128)(2,1)S(1)}, s32[8,8,128]{2,1,0:T(8,128)...) custom-call(s32[8]{0:T(128)} %owner_hbm.1, ...), custom_call_target="tpu_custom_call" | custom-call | flops 134217728 | bytes 3145728 | tf_op jit(solution)/shard_map/pack/pallas_call | solution.py:105
  3.1 3.1 %collective-permute-start = (bf16[2,128,512]{2,1,0:T(8,128)(2,1)S(1)}, bf16[2,128,512]{2,1,0:T(8,128)(2,1)S(1)}, u32[]{:S(2)}, u32[]{:S(2)}) collective-permute-start(bf16[2,128,512]{2,1,0:T(8,128)(2,1)S(1)} %get-tuple-element.16), channel_id=1, source_target_pairs={{0,1},{1,2},{2,3},{3,4},{4,5},{5,6},{6,7},{7,8},{8,9},{9,10},{10,1... | collective-permute-start | bytes 786440 | tf_op jit(solution)/shard_map/ppermute | solution.py:450
  6.2 3.7 %collective-permute-start.1 = (bf16[2,128,512]{2,1,0:T(8,128)(2,1)}, bf16[2,128,512]{2,1,0:T(8,128)(2,1)S(1)}, u32[]{:S(2)}, u32[]{:S(2)}) collective-permute-start(bf16[2,128,512]{2,1,0:T(8,128)(2,1)} %get-tuple-element.24), channel_id=1, source_target_pairs={{1,0},{2,1},{3,2},{4,3},{5,4},{6,5},{7,6},{8,7},{9,8},{10,9},{11,1... | collective-permute-start | bytes 786440 | tf_op jit(solution)/shard_map/ppermute | solution.py:451
  10.0 5.8 %all-to-all-start = ((bf16[16,9,16,128]{3,2,1,0:T(8,128)(2,1)}), bf16[16,9,16,128]{3,2,1,0:T(8,128)(2,1)S(1)}, u32[]{:S(2)}, u32[]{:S(2)}) async-start(bf16[16,9,16,128]{3,2,1,0:T(8,128)(2,1)} %get-tuple-element.19), calls=%async_computation | async-start | bytes 1179648 | tf_op jit(solution)/shard_map/all_to_all | solution.py:454
  16.4 0.0 collective-permute-done.refs_3_
  16.4 0.0 collective-permute-done.1.refs_4_
  16.4 5.1 %fine.1.partial_ref = bf16[8,128,512]{2,1,0:T(8,128)(2,1)S(1)} custom-call(s32[1]{0:T(128)} %bitcast.late_ref, s32[56]{0:T(128)} %refs_0_.3, s32[56]{0:T(128)} %refs_1_.3, s32[1]{0:T(128)S(6)} %copy.18.refs_2_, bf16[2,128,512]{2,1,0:T(8,128)(2,1)S(1)} %collective-permute-done.refs_3_, bf16[2,128,512]{2,1,0:T(8,128)(2,1)S(1)} %collective-permute-done.1.refs_4_, ...), custom_call_target="tpu_custom_call" | custom-call | flops 137438953472 | bytes 1048576 | tf_op jit(solution)/shard_map/fine/pallas_call | solution.py:352
  21.5 0.7 %collective-permute-start.2 = (bf16[2,128,512]{2,1,0:T(8,128)(2,1)}, bf16[2,128,512]{2,1,0:T(8,128)(2,1)S(1)}, u32[]{:S(2)}, u32[]{:S(2)}) collective-permute-start(bf16[2,128,512]{2,1,0:T(8,128)(2,1)} %get-tuple-element.24), channel_id=1, source_target_pairs={{64,63},{128,127},{192,191},{256,255},{320,319},{384,383},{448,447}} | collective-permute-start | bytes 786440 | tf_op jit(solution)/shard_map/ppermute | solution.py:459
  22.2 4.8 %all-to-all-done.arrived_ref = bf16[16,9,16,128]{3,2,1,0:T(8,128)(2,1)S(1)} async-done(((bf16[16,9,16,128]{3,2,1,0:T(8,128)(2,1)}), bf16[16,9,16,128]{3,2,1,0:T(8,128)(2,1)S(1)}, u32[]{:S(2)}, u32[]{:S(2)}) %all-to-all-start) | async-done | bytes 589856 | tf_op jit(solution)/shard_map/all_to_all | solution.py:454
  27.0 1.8 %coarse.1 = bf16[4,2,16,512]{3,2,1,0:T(8,128)(2,1)S(1)} custom-call(s32[1]{0:T(128)} %bitcast.3.sub_ref, s32[2]{0:T(128)} %offset_hbm.1, bf16[512,512]{1,0:T(8,128)(2,1)} %second_hbm.1, bf16[16,9,16,128]{3,2,1,0:T(8,128)(2,1)S(1)} %all-to-all-done.arrived_ref, bf16[1024,512]{1,0:T(8,128)(2,1)S(1)} %get-tuple-element.20.first_ref, ...), custom_call_target="tpu_custom_call" | custom-call | flops 536870912 | bytes 3145728 | tf_op jit(solution)/shard_map/coarse/pallas_call | solution.py:205
  28.9 9.2 %all-gather = bf16[16,2,16,512]{3,2,1,0:T(8,128)(2,1)S(1)} all-gather(bf16[4,2,16,512]{3,2,1,0:T(8,128)(2,1)S(1)} %coarse.1), channel_id=2, replica_groups=mesh['win'=32,'mem'=4,'sub'=4] {'mem'}, dimensions={0}, use_global_device_ids=true | all-gather | bytes 655360 | tf_op jit(solution)/shard_map/all_gather | solution.py:461
  38.0 0.0 collective-permute-done.2.refs_4_
  38.0 1.3 %finish.1 = bf16[8,128,512]{2,1,0:T(8,128)(2,1)} custom-call(s32[1]{0:T(128)} %bitcast.late_ref, s32[1]{0:T(128)} %bitcast.1.mem_ref, bf16[8,128,512]{2,1,0:T(8,128)(2,1)S(1)} %fine.1.partial_ref, s32[8,8,128]{2,1,0:T(8,128)S(1)} %get-tuple-element.18.slot_ref, bf16[4,4,2,16,512]{4,3,2,1,0:T(8,128)(2,1)S(1)} %bitcast.6, s32[56]{0:T(128)} %refs_0_.3, ...), custom_call_target="tpu_custom_call" | custom-call | flops 33554432 | bytes 4194304 | tf_op jit(solution)/shard_map/finish/pallas_call | solution.py:397
Async XLA Ops:
  3.1 13.3 %collective-permute-start = (bf16[2,128,512]{2,1,0:T(8,128)(2,1)S(1)}, bf16[2,128,512]{2,1,0:T(8,128)(2,1)S(1)}, u32[]{:S(2)}, u32[]{:S(2)}) collective-permute-start(bf16[2,128,512]{2,1,0:T(8,128)(2,1)S(1)} %get-tuple-element.16), channel_id=1, source_target_pairs={{0,1},{1,2},{2,3},{3,4},{4,5},{5,6},{6,7},{7,8},{8,9},{9,10},{10,1... | collective-permute-start | bytes 786440 | tf_op jit(solution)/shard_map/ppermute | solution.py:450
  6.2 10.2 %collective-permute-start.1 = (bf16[2,128,512]{2,1,0:T(8,128)(2,1)}, bf16[2,128,512]{2,1,0:T(8,128)(2,1)S(1)}, u32[]{:S(2)}, u32[]{:S(2)}) collective-permute-start(bf16[2,128,512]{2,1,0:T(8,128)(2,1)} %get-tuple-element.24), channel_id=1, source_target_pairs={{1,0},{2,1},{3,2},{4,3},{5,4},{6,5},{7,6},{8,7},{9,8},{10,9},{11,1... | collective-permute-start | bytes 786440 | tf_op jit(solution)/shard_map/ppermute | solution.py:451
  10.0 17.1 %all-to-all-start = ((bf16[16,9,16,128]{3,2,1,0:T(8,128)(2,1)}), bf16[16,9,16,128]{3,2,1,0:T(8,128)(2,1)S(1)}, u32[]{:S(2)}, u32[]{:S(2)}) async-start(bf16[16,9,16,128]{3,2,1,0:T(8,128)(2,1)} %get-tuple-element.19), calls=%async_computation | async-start | bytes 1179648 | tf_op jit(solution)/shard_map/all_to_all | solution.py:454
  21.5 16.5 %collective-permute-start.2 = (bf16[2,128,512]{2,1,0:T(8,128)(2,1)}, bf16[2,128,512]{2,1,0:T(8,128)(2,1)S(1)}, u32[]{:S(2)}, u32[]{:S(2)}) collective-permute-start(bf16[2,128,512]{2,1,0:T(8,128)(2,1)} %get-tuple-element.24), channel_id=1, source_target_pairs={{64,63},{128,127},{192,191},{256,255},{320,319},{384,383},{448,447}} | collective-permute-start | bytes 786440 | tf_op jit(solution)/shard_map/ppermute | solution.py:459

commit v5 on v4

--- a/solution.py
+++ b/solution.py
@@ -9,6 +9,7 @@
 POOL = 8
 WIN = 4
 ROW = 64
+PARTS = 2
 DEPTH = 2
 SIDE = 4
 F32 = jnp.float32
@@ -58,7 +59,8 @@
     subs = send_ref.shape[0] // WIN
     halo = lower_ref.shape[0]
     ints = started([(owner_hbm, owner_ref), (halo_hbm, halo_ref)], int_sems)
-    loads = started([(nodes_hbm.at[k], nodes_ref.at[k]) for k in range(blocks)], node_sems)
+    parts = [pl.ds(at, blocks // PARTS) for at in range(0, blocks, blocks // PARTS)]
+    loads = started([(nodes_hbm.at[part], nodes_ref.at[part]) for part in parts], node_sems)
     held = started(
         [
             (first_hbm, first_ref),
@@ -68,8 +70,9 @@
         ],
         held_sems,
     )
-    row = lax.broadcasted_iota(jnp.int32, (tile, rows), 0)
-    col = lax.broadcasted_iota(jnp.int32, (tile, rows), 1)
+    few = blocks // PARTS
+    row = lax.broadcasted_iota(jnp.int32, (few * tile, few * rows), 0)
+    col = lax.broadcasted_iota(jnp.int32, (few * tile, few * rows), 1)
     average = jnp.where(col // POOL == row, 1.0 / POOL, 0.0).astype(BF16)
     for copy in ints:
         copy.wait()
@@ -83,12 +86,15 @@
         tag = tag.astype(F32).astype(BF16)
         for s in range(subs):
             send_ref[d * subs + s, groups * 2] = tag
-    for k, (d, r) in enumerate(slots):
-        loads[k].wait()
-        pooled = jnp.dot(average, nodes_ref[k], preferred_element_type=F32).astype(BF16)
-        for s in range(subs):
-            for c in range(groups):
-                send_ref[d * subs + s, c * 2 + r] = pooled[:, c * lanes : (c + 1) * lanes]
+    for part, load in enumerate(loads):
+        load.wait()
+        nodes = nodes_ref[part * few : (part + 1) * few].reshape(few * rows, width)
+        pooled = jnp.dot(average, nodes, preferred_element_type=F32).astype(BF16)
+        for k, (d, r) in enumerate(slots[part * few : (part + 1) * few]):
+            for s in range(subs):
+                for c in range(groups):
+                    piece = pooled[k * tile : (k + 1) * tile, c * lanes : (c + 1) * lanes]
+                    send_ref[d * subs + s, c * 2 + r] = piece
     for h in range(halo):
         lower_ref[h] = nodes_ref[halo_ref[h]]
         upper_ref[h] = nodes_ref[halo_ref[halo + h]]
@@ -124,7 +130,7 @@
             pltpu.SMEM((WIN,), jnp.int32),
             pltpu.SMEM((2 * WIN,), jnp.int32),
             pltpu.SemaphoreType.DMA((2,)),
-            pltpu.SemaphoreType.DMA((count,)),
+            pltpu.SemaphoreType.DMA((PARTS,)),
             pltpu.SemaphoreType.DMA((4,)),
         ],
         compiler_params=PARAMS,

time: 39.6 us -> 40.7 us (1.028)
  the two profiles are of different devices: /device:TPU:41 before, /device:TPU:495 now
where the time goes in v5:
time: 40.7 us; the launch traced here: 40.4 us
  starting transfers between devices  13.2 us (32%)
  Pallas kernels  12.5 us (31%)
  blocking collectives  7.56 us (19%)
  waiting for transfers between devices  6.48 us (16%)
  between operations  0.72 us (2%)
    pallas_call x1, Pallas kernels, finish(): pl.pallas_call(finish_kernel, name='finish', out_shape=jax.ShapeDtypeStru...  7.76 us
    all_gather x1, blocking collectives, per_device(): replies = lax.all_gather(reply, 'mem')  7.56 us
    all_to_all x1, starting transfers between devices, per_device(): arrived = lax.all_to_all(send, ('mem', 'sub'), 0, 0, tiled=True)  6.62 us
    all_to_all x1, waiting for transfers between devices, per_device(): arrived = lax.all_to_all(send, ('mem', 'sub'), 0, 0, tiled=True)  6.47 us
    ppermute x1, starting transfers between devices, per_device(): lax.ppermute(lower, everyone, [(i + 1, i) for i in range(devices - 1) if...  3.37 us
    pallas_call x1, Pallas kernels, pack(): pl.pallas_call(pack_kernel, name='pack', out_shape=(jax.ShapeDtypeStruct(...  2.8 us
    ppermute x1, starting transfers between devices, per_device(): lax.ppermute(upper, everyone, [(i, i + 1) for i in range(devices - 1)])  1.92 us
    pallas_call x1, Pallas kernels, coarse_update(): pl.pallas_call(coarse_kernel, name='coarse', out_shape=jax.ShapeDtypeStru...  1.8 us
  transfers between devices with their start and end apart: 4, of which 1 were waited for; matrix products, arithmetic and copies ran while one was open for 0% of the time, Pallas kernels for 5%

profile of v5, /device:TPU:495, one launch (start us, length us, event | category | flops | bytes accessed | tf_op | source)
XLA Modules:
  0.0 40.4 jit_solution(496602867204562989)
XLA Ops:
  0.0 2.8 %pack.1 = (bf16[16,9,16,128]{3,2,1,0:T(8,128)(2,1)}, bf16[2,128,512]{2,1,0:T(8,128)(2,1)}, bf16[2,128,512]{2,1,0:T(8,128)(2,1)S(1)}, s32[8,8,128]{2,1,0:T(8,128)...) custom-call(s32[8]{0:T(128)} %owner_hbm.1, ...), custom_call_target="tpu_custom_call" | custom-call | flops 134217728 | bytes 3145728 | tf_op jit(solution)/shard_map/pack/pallas_call | solution.py:111
  2.8 1.9 %collective-permute-start = (bf16[2,128,512]{2,1,0:T(8,128)(2,1)S(1)}, bf16[2,128,512]{2,1,0:T(8,128)(2,1)S(1)}, u32[]{:S(2)}, u32[]{:S(2)}) collective-permute-start(bf16[2,128,512]{2,1,0:T(8,128)(2,1)S(1)} %get-tuple-element.16), channel_id=1, source_target_pairs={{0,1},{1,2},{2,3},{3,4},{4,5},{5,6},{6,7},{7,8},{8,9},{9,10},{10,1... | collective-permute-start | bytes 786440 | tf_op jit(solution)/shard_map/ppermute | solution.py:456
  4.7 3.4 %collective-permute-start.1 = (bf16[2,128,512]{2,1,0:T(8,128)(2,1)}, bf16[2,128,512]{2,1,0:T(8,128)(2,1)S(1)}, u32[]{:S(2)}, u32[]{:S(2)}) collective-permute-start(bf16[2,128,512]{2,1,0:T(8,128)(2,1)} %get-tuple-element.24), channel_id=1, source_target_pairs={{1,0},{2,1},{3,2},{4,3},{5,4},{6,5},{7,6},{8,7},{9,8},{10,9},{11,1... | collective-permute-start | bytes 786440 | tf_op jit(solution)/shard_map/ppermute | solution.py:457
  8.1 6.6 %all-to-all-start = ((bf16[16,9,16,128]{3,2,1,0:T(8,128)(2,1)}), bf16[16,9,16,128]{3,2,1,0:T(8,128)(2,1)S(1)}, u32[]{:S(2)}, u32[]{:S(2)}) async-start(bf16[16,9,16,128]{3,2,1,0:T(8,128)(2,1)} %get-tuple-element.19), calls=%async_computation | async-start | bytes 1179648 | tf_op jit(solution)/shard_map/all_to_all | solution.py:460
  15.4 0.0 collective-permute-done.refs_3_
  15.4 0.0 collective-permute-done.1.refs_4_
  15.4 0.1 fine.1.partial_ref
  15.5 1.3 %collective-permute-start.2 = (bf16[2,128,512]{2,1,0:T(8,128)(2,1)}, bf16[2,128,512]{2,1,0:T(8,128)(2,1)S(1)}, u32[]{:S(2)}, u32[]{:S(2)}) collective-permute-start(bf16[2,128,512]{2,1,0:T(8,128)(2,1)} %get-tuple-element.24), channel_id=1, source_target_pairs={{64,63},{128,127},{192,191},{256,255},{320,319},{384,383},{448,447}} | collective-permute-start | bytes 786440 | tf_op jit(solution)/shard_map/ppermute | solution.py:465
  16.8 6.5 %all-to-all-done.arrived_ref = bf16[16,9,16,128]{3,2,1,0:T(8,128)(2,1)S(1)} async-done(((bf16[16,9,16,128]{3,2,1,0:T(8,128)(2,1)}), bf16[16,9,16,128]{3,2,1,0:T(8,128)(2,1)S(1)}, u32[]{:S(2)}, u32[]{:S(2)}) %all-to-all-start) | async-done | bytes 589856 | tf_op jit(solution)/shard_map/all_to_all | solution.py:460
  23.3 1.8 %coarse.1 = bf16[4,2,16,512]{3,2,1,0:T(8,128)(2,1)S(1)} custom-call(s32[1]{0:T(128)} %bitcast.3.sub_ref, s32[2]{0:T(128)} %offset_hbm.1, bf16[512,512]{1,0:T(8,128)(2,1)} %second_hbm.1, bf16[16,9,16,128]{3,2,1,0:T(8,128)(2,1)S(1)} %all-to-all-done.arrived_ref, bf16[1024,512]{1,0:T(8,128)(2,1)S(1)} %get-tuple-element.20.first_ref, ...), custom_call_target="tpu_custom_call" | custom-call | flops 536870912 | bytes 3145728 | tf_op jit(solution)/shard_map/coarse/pallas_call | solution.py:211
  25.1 7.6 %all-gather = bf16[16,2,16,512]{3,2,1,0:T(8,128)(2,1)S(1)} all-gather(bf16[4,2,16,512]{3,2,1,0:T(8,128)(2,1)S(1)} %coarse.1), channel_id=2, replica_groups=mesh['win'=32,'mem'=4,'sub'=4] {'mem'}, dimensions={0}, use_global_device_ids=true | all-gather | bytes 655360 | tf_op jit(solution)/shard_map/all_gather | solution.py:467
  32.7 0.0 collective-permute-done.2.refs_4_
  32.7 7.8 %finish.1 = bf16[8,128,512]{2,1,0:T(8,128)(2,1)} custom-call(s32[1]{0:T(128)} %bitcast.late_ref, s32[1]{0:T(128)} %bitcast.1.mem_ref, bf16[8,128,512]{2,1,0:T(8,128)(2,1)S(1)} %fine.1.partial_ref, s32[8,8,128]{2,1,0:T(8,128)S(1)} %get-tuple-element.18.slot_ref, bf16[4,4,2,16,512]{4,3,2,1,0:T(8,128)(2,1)S(1)} %bitcast.6, s32[56]{0:T(128)} %refs_0_.3, ...), custom_call_target="tpu_custom_call" | custom-call | flops 33554432 | bytes 4194304 | tf_op jit(solution)/shard_map/finish/pallas_call | solution.py:403
Async XLA Ops:
  2.8 12.6 %collective-permute-start = (bf16[2,128,512]{2,1,0:T(8,128)(2,1)S(1)}, bf16[2,128,512]{2,1,0:T(8,128)(2,1)S(1)}, u32[]{:S(2)}, u32[]{:S(2)}) collective-permute-start(bf16[2,128,512]{2,1,0:T(8,128)(2,1)S(1)} %get-tuple-element.16), channel_id=1, source_target_pairs={{0,1},{1,2},{2,3},{3,4},{4,5},{5,6},{6,7},{7,8},{8,9},{9,10},{10,1... | collective-permute-start | bytes 786440 | tf_op jit(solution)/shard_map/ppermute | solution.py:456
  4.7 10.7 %collective-permute-start.1 = (bf16[2,128,512]{2,1,0:T(8,128)(2,1)}, bf16[2,128,512]{2,1,0:T(8,128)(2,1)S(1)}, u32[]{:S(2)}, u32[]{:S(2)}) collective-permute-start(bf16[2,128,512]{2,1,0:T(8,128)(2,1)} %get-tuple-element.24), channel_id=1, source_target_pairs={{1,0},{2,1},{3,2},{4,3},{5,4},{6,5},{7,6},{8,7},{9,8},{10,9},{11,1... | collective-permute-start | bytes 786440 | tf_op jit(solution)/shard_map/ppermute | solution.py:457
  8.1 15.2 %all-to-all-start = ((bf16[16,9,16,128]{3,2,1,0:T(8,128)(2,1)}), bf16[16,9,16,128]{3,2,1,0:T(8,128)(2,1)S(1)}, u32[]{:S(2)}, u32[]{:S(2)}) async-start(bf16[16,9,16,128]{3,2,1,0:T(8,128)(2,1)} %get-tuple-element.19), calls=%async_computation | async-start | bytes 1179648 | tf_op jit(solution)/shard_map/all_to_all | solution.py:460
  15.5 17.1 %collective-permute-start.2 = (bf16[2,128,512]{2,1,0:T(8,128)(2,1)}, bf16[2,128,512]{2,1,0:T(8,128)(2,1)S(1)}, u32[]{:S(2)}, u32[]{:S(2)}) collective-permute-start(bf16[2,128,512]{2,1,0:T(8,128)(2,1)} %get-tuple-element.24), channel_id=1, source_target_pairs={{64,63},{128,127},{192,191},{256,255},{320,319},{384,383},{448,447}} | collective-permute-start | bytes 786440 | tf_op jit(solution)/shard_map/ppermute | solution.py:465

commit v6 on v5

--- a/solution.py
+++ b/solution.py
@@ -49,15 +49,16 @@
 
 def pack_kernel(
     owner_hbm, halo_hbm, nodes_hbm, first_hbm, tiles_hbm, bias_hbm, gain_hbm,
-    send_ref, lower_ref, upper_ref, slot_ref, first_ref, tiles_ref, bias_ref, gain_ref,
-    owner_ref, halo_ref, nodes_ref, count_ref, index_ref, int_sems, node_sems, held_sems,
+    send_hbm, lower_hbm, upper_ref, slot_ref, first_ref, tiles_ref, bias_ref, gain_ref,
+    owner_ref, halo_ref, nodes_ref, send_ref, count_ref, index_ref,
+    int_sems, node_sems, held_sems, lower_sems, send_sems,
 ):
     blocks, rows, width = nodes_ref.shape
     tile = rows // POOL
     lanes = send_ref.shape[-1]
     groups = width // lanes
-    subs = send_ref.shape[0] // WIN
-    halo = lower_ref.shape[0]
+    subs = send_hbm.shape[0] // WIN
+    halo = upper_ref.shape[0]
     ints = started([(owner_hbm, owner_ref), (halo_hbm, halo_ref)], int_sems)
     parts = [pl.ds(at, blocks // PARTS) for at in range(0, blocks, blocks // PARTS)]
     loads = started([(nodes_hbm.at[part], nodes_ref.at[part]) for part in parts], node_sems)
@@ -84,21 +85,24 @@
     for d in range(WIN):
         tag = jnp.where((lane // tile) % 2 == 0, index_ref[2 * d], index_ref[2 * d + 1])
         tag = tag.astype(F32).astype(BF16)
-        for s in range(subs):
-            send_ref[d * subs + s, groups * 2] = tag
+        send_ref[d, groups * 2] = tag
+    outs = []
     for part, load in enumerate(loads):
         load.wait()
+        if part == PARTS - 1:
+            outs += started([(nodes_ref.at[halo_ref[h]], lower_hbm.at[h]) for h in range(halo)], lower_sems)
         nodes = nodes_ref[part * few : (part + 1) * few].reshape(few * rows, width)
         pooled = jnp.dot(average, nodes, preferred_element_type=F32).astype(BF16)
         for k, (d, r) in enumerate(slots[part * few : (part + 1) * few]):
-            for s in range(subs):
-                for c in range(groups):
-                    piece = pooled[k * tile : (k + 1) * tile, c * lanes : (c + 1) * lanes]
-                    send_ref[d * subs + s, c * 2 + r] = piece
+            for c in range(groups):
+                piece = pooled[k * tile : (k + 1) * tile, c * lanes : (c + 1) * lanes]
+                send_ref[d, c * 2 + r] = piece
+    outs += started(
+        [(send_ref.at[d], send_hbm.at[d * subs + s]) for d in range(WIN) for s in range(subs)], send_sems
+    )
     for h in range(halo):
-        lower_ref[h] = nodes_ref[halo_ref[h]]
         upper_ref[h] = nodes_ref[halo_ref[halo + h]]
-    for copy in held:
+    for copy in held + outs:
         copy.wait()
 
 
@@ -122,16 +126,19 @@
             jax.ShapeDtypeStruct((1, width), F32),
         ),
         in_specs=[HBM_SPEC] * 7,
-        out_specs=(VMEM_SPEC,) * 8,
+        out_specs=(ANY_SPEC,) * 2 + (VMEM_SPEC,) * 6,
         scratch_shapes=[
             pltpu.SMEM((count,), jnp.int32),
             pltpu.SMEM((halos,), jnp.int32),
             pltpu.VMEM(blocks.shape, BF16),
+            pltpu.VMEM((WIN, pieces, tile, lanes), BF16),
             pltpu.SMEM((WIN,), jnp.int32),
             pltpu.SMEM((2 * WIN,), jnp.int32),
             pltpu.SemaphoreType.DMA((2,)),
             pltpu.SemaphoreType.DMA((PARTS,)),
             pltpu.SemaphoreType.DMA((4,)),
+            pltpu.SemaphoreType.DMA((halos // 2,)),
+            pltpu.SemaphoreType.DMA((WIN * subs,)),
         ],
         compiler_params=PARAMS,
         cost_estimate=pl.CostEstimate(flops=1 << 27, bytes_accessed=3 << 20, transcendentals=0),

time: 40.7 us -> 39.5 us (0.971)
  the two profiles are of different devices: /device:TPU:495 before, /device:TPU:57 now
where the time goes in v6:
time: 39.5 us; the launch traced here: 39.1 us
  starting transfers between devices  13.3 us (34%)
  Pallas kernels  11.1 us (28%)
  blocking collectives  9.17 us (23%)
  waiting for transfers between devices  4.8 us (12%)
  between operations  0.72 us (2%)
    all_gather x1, blocking collectives, per_device(): replies = lax.all_gather(reply, 'mem')  9.17 us
    all_to_all x1, starting transfers between devices, per_device(): arrived = lax.all_to_all(send, ('mem', 'sub'), 0, 0, tiled=True)  5.78 us
    pallas_call x1, Pallas kernels, fine_update(): pl.pallas_call(fine_kernel, name='fine', out_shape=jax.ShapeDtypeStruct(n...  5.14 us
    all_to_all x1, waiting for transfers between devices, per_device(): arrived = lax.all_to_all(send, ('mem', 'sub'), 0, 0, tiled=True)  4.79 us
    ppermute x1, starting transfers between devices, per_device(): lax.ppermute(lower, everyone, [(i + 1, i) for i in range(devices - 1) if...  3.75 us
    ppermute x1, starting transfers between devices, per_device(): lax.ppermute(upper, everyone, [(i, i + 1) for i in range(devices - 1)])  3.12 us
    pallas_call x1, Pallas kernels, pack(): pl.pallas_call(pack_kernel, name='pack', out_shape=(jax.ShapeDtypeStruct(...  2.84 us
    pallas_call x1, Pallas kernels, coarse_update(): pl.pallas_call(coarse_kernel, name='coarse', out_shape=jax.ShapeDtypeStru...  1.8 us
  transfers between devices with their start and end apart: 4, of which 1 were waited for; matrix products, arithmetic and copies ran while one was open for 0% of the time, Pallas kernels for 18%

profile of v6, /device:TPU:57, one launch (start us, length us, event | category | flops | bytes accessed | tf_op | source)
XLA Modules:
  0.0 39.1 jit_solution(12153898190004067711)
XLA Ops:
  0.0 2.8 %pack.1 = (bf16[16,9,16,128]{3,2,1,0:T(8,128)(2,1)}, bf16[2,128,512]{2,1,0:T(8,128)(2,1)}, bf16[2,128,512]{2,1,0:T(8,128)(2,1)S(1)}, s32[8,8,128]{2,1,0:T(8,128)...) custom-call(s32[8]{0:T(128)} %owner_hbm.1, ...), custom_call_target="tpu_custom_call" | custom-call | flops 134217728 | bytes 3145728 | tf_op jit(solution)/shard_map/pack/pallas_call | solution.py:115
  2.8 3.1 %collective-permute-start = (bf16[2,128,512]{2,1,0:T(8,128)(2,1)S(1)}, bf16[2,128,512]{2,1,0:T(8,128)(2,1)S(1)}, u32[]{:S(2)}, u32[]{:S(2)}) collective-permute-start(bf16[2,128,512]{2,1,0:T(8,128)(2,1)S(1)} %get-tuple-element.16), channel_id=1, source_target_pairs={{0,1},{1,2},{2,3},{3,4},{4,5},{5,6},{6,7},{7,8},{8,9},{9,10},{10,1... | collective-permute-start | bytes 786440 | tf_op jit(solution)/shard_map/ppermute | solution.py:463
  6.0 3.7 %collective-permute-start.1 = (bf16[2,128,512]{2,1,0:T(8,128)(2,1)}, bf16[2,128,512]{2,1,0:T(8,128)(2,1)S(1)}, u32[]{:S(2)}, u32[]{:S(2)}) collective-permute-start(bf16[2,128,512]{2,1,0:T(8,128)(2,1)} %get-tuple-element.24), channel_id=1, source_target_pairs={{1,0},{2,1},{3,2},{4,3},{5,4},{6,5},{7,6},{8,7},{9,8},{10,9},{11,1... | collective-permute-start | bytes 786440 | tf_op jit(solution)/shard_map/ppermute | solution.py:464
  9.7 5.8 %all-to-all-start = ((bf16[16,9,16,128]{3,2,1,0:T(8,128)(2,1)}), bf16[16,9,16,128]{3,2,1,0:T(8,128)(2,1)S(1)}, u32[]{:S(2)}, u32[]{:S(2)}) async-start(bf16[16,9,16,128]{3,2,1,0:T(8,128)(2,1)} %get-tuple-element.19), calls=%async_computation | async-start | bytes 1179648 | tf_op jit(solution)/shard_map/all_to_all | solution.py:467
  16.2 0.0 collective-permute-done.refs_3_
  16.2 0.0 collective-permute-done.1.refs_4_
  16.2 5.1 %fine.1.partial_ref = bf16[8,128,512]{2,1,0:T(8,128)(2,1)S(1)} custom-call(s32[1]{0:T(128)} %bitcast.late_ref, s32[56]{0:T(128)} %refs_0_.3, s32[56]{0:T(128)} %refs_1_.3, s32[1]{0:T(128)S(6)} %copy.18.refs_2_, bf16[2,128,512]{2,1,0:T(8,128)(2,1)S(1)} %collective-permute-done.refs_3_, bf16[2,128,512]{2,1,0:T(8,128)(2,1)S(1)} %collective-permute-done.1.refs_4_, ...), custom_call_target="tpu_custom_call" | custom-call | flops 137438953472 | bytes 1048576 | tf_op jit(solution)/shard_map/fine/pallas_call | solution.py:365
  21.3 0.7 %collective-permute-start.2 = (bf16[2,128,512]{2,1,0:T(8,128)(2,1)}, bf16[2,128,512]{2,1,0:T(8,128)(2,1)S(1)}, u32[]{:S(2)}, u32[]{:S(2)}) collective-permute-start(bf16[2,128,512]{2,1,0:T(8,128)(2,1)} %get-tuple-element.24), channel_id=1, source_target_pairs={{64,63},{128,127},{192,191},{256,255},{320,319},{384,383},{448,447}} | collective-permute-start | bytes 786440 | tf_op jit(solution)/shard_map/ppermute | solution.py:472
  22.0 4.8 %all-to-all-done.arrived_ref = bf16[16,9,16,128]{3,2,1,0:T(8,128)(2,1)S(1)} async-done(((bf16[16,9,16,128]{3,2,1,0:T(8,128)(2,1)}), bf16[16,9,16,128]{3,2,1,0:T(8,128)(2,1)S(1)}, u32[]{:S(2)}, u32[]{:S(2)}) %all-to-all-start) | async-done | bytes 589856 | tf_op jit(solution)/shard_map/all_to_all | solution.py:467
  26.8 1.8 %coarse.1 = bf16[4,2,16,512]{3,2,1,0:T(8,128)(2,1)S(1)} custom-call(s32[1]{0:T(128)} %bitcast.3.sub_ref, s32[2]{0:T(128)} %offset_hbm.1, bf16[512,512]{1,0:T(8,128)(2,1)} %second_hbm.1, bf16[16,9,16,128]{3,2,1,0:T(8,128)(2,1)S(1)} %all-to-all-done.arrived_ref, bf16[1024,512]{1,0:T(8,128)(2,1)S(1)} %get-tuple-element.20.first_ref, ...), custom_call_target="tpu_custom_call" | custom-call | flops 536870912 | bytes 3145728 | tf_op jit(solution)/shard_map/coarse/pallas_call | solution.py:218
  28.6 9.2 %all-gather = bf16[16,2,16,512]{3,2,1,0:T(8,128)(2,1)S(1)} all-gather(bf16[4,2,16,512]{3,2,1,0:T(8,128)(2,1)S(1)} %coarse.1), channel_id=2, replica_groups=mesh['win'=32,'mem'=4,'sub'=4] {'mem'}, dimensions={0}, use_global_device_ids=true | all-gather | bytes 655360 | tf_op jit(solution)/shard_map/all_gather | solution.py:474
  37.8 0.0 collective-permute-done.2.refs_4_
  37.8 1.3 %finish.1 = bf16[8,128,512]{2,1,0:T(8,128)(2,1)} custom-call(s32[1]{0:T(128)} %bitcast.late_ref, s32[1]{0:T(128)} %bitcast.1.mem_ref, bf16[8,128,512]{2,1,0:T(8,128)(2,1)S(1)} %fine.1.partial_ref, s32[8,8,128]{2,1,0:T(8,128)S(1)} %get-tuple-element.18.slot_ref, bf16[4,4,2,16,512]{4,3,2,1,0:T(8,128)(2,1)S(1)} %bitcast.6, s32[56]{0:T(128)} %refs_0_.3, ...), custom_call_target="tpu_custom_call" | custom-call | flops 33554432 | bytes 4194304 | tf_op jit(solution)/shard_map/finish/pallas_call | solution.py:410
Async XLA Ops:
  2.8 13.3 %collective-permute-start = (bf16[2,128,512]{2,1,0:T(8,128)(2,1)S(1)}, bf16[2,128,512]{2,1,0:T(8,128)(2,1)S(1)}, u32[]{:S(2)}, u32[]{:S(2)}) collective-permute-start(bf16[2,128,512]{2,1,0:T(8,128)(2,1)S(1)} %get-tuple-element.16), channel_id=1, source_target_pairs={{0,1},{1,2},{2,3},{3,4},{4,5},{5,6},{6,7},{7,8},{8,9},{9,10},{10,1... | collective-permute-start | bytes 786440 | tf_op jit(solution)/shard_map/ppermute | solution.py:463
  6.0 10.2 %collective-permute-start.1 = (bf16[2,128,512]{2,1,0:T(8,128)(2,1)}, bf16[2,128,512]{2,1,0:T(8,128)(2,1)S(1)}, u32[]{:S(2)}, u32[]{:S(2)}) collective-permute-start(bf16[2,128,512]{2,1,0:T(8,128)(2,1)} %get-tuple-element.24), channel_id=1, source_target_pairs={{1,0},{2,1},{3,2},{4,3},{5,4},{6,5},{7,6},{8,7},{9,8},{10,9},{11,1... | collective-permute-start | bytes 786440 | tf_op jit(solution)/shard_map/ppermute | solution.py:464
  9.7 17.1 %all-to-all-start = ((bf16[16,9,16,128]{3,2,1,0:T(8,128)(2,1)}), bf16[16,9,16,128]{3,2,1,0:T(8,128)(2,1)S(1)}, u32[]{:S(2)}, u32[]{:S(2)}) async-start(bf16[16,9,16,128]{3,2,1,0:T(8,128)(2,1)} %get-tuple-element.19), calls=%async_computation | async-start | bytes 1179648 | tf_op jit(solution)/shard_map/all_to_all | solution.py:467
  21.3 16.5 %collective-permute-start.2 = (bf16[2,128,512]{2,1,0:T(8,128)(2,1)}, bf16[2,128,512]{2,1,0:T(8,128)(2,1)S(1)}, u32[]{:S(2)}, u32[]{:S(2)}) collective-permute-start(bf16[2,128,512]{2,1,0:T(8,128)(2,1)} %get-tuple-element.24), channel_id=1, source_target_pairs={{64,63},{128,127},{192,191},{256,255},{320,319},{384,383},{448,447}} | collective-permute-start | bytes 786440 | tf_op jit(solution)/shard_map/ppermute | solution.py:472
